TPU v7x, 256 devices: a whole 4x4x8 slice. The times are simulated.
256 devices in a mesh: rows: 32 (over z_hi, x, core), cols: 8 (over y, z_lo).
Axes of the slice: x: 4, y: 4, z: 8 (z_hi: 4, z_lo: 2; z = z_hi * 2 + z_lo), core: 2. Of those that a mesh axis runs over, the one named last changes fastest.
Arguments:
- xin: bfloat16 [256, 512, 1024], P('rows', 'cols'), may hold values from -6 to 6
- gate_in: bfloat16 [256, 512, 1024], P('rows', 'cols'), may hold values from -6 to 6
- w_proj: bfloat16 [1024, 128], replicated, may hold values from -0.1875 to 0.1875
- rate: float32 [4, 16], replicated, may hold values from 0.0001953125 to 0.05
- skip: float32 [1024], replicated, may hold values from 0.5 to 1.5
- norm_gain: float32 [1024], replicated, may hold values from 0.5 to 1.5
- w_out: bfloat16 [1024, 512], replicated, may hold values from -0.1875 to 0.1875
Outputs:
- mixed: bfloat16 [256, 512, 512], P('rows', 'cols')
All inputs are finite; a program needn't handle non-finite values.
Results may differ from a plain program's by a relative error of at most 0.0049.
Values sent between devices are 32-bit elements; how exact they have to be, the bound alone decides.
A program may use at most 192 MiB of HBM per device.

v0:
```python
import jax
import jax.numpy as jnp
from jax import lax
from jax.sharding import PartitionSpec as P


def passed_along(block, axis, distance):
    devices = range(lax.axis_size(axis))
    route = [(i - distance, i) for i in devices if i - distance in devices]
    return lax.ppermute(block, axis, route)


def line_scan(weighted, logdec, outcoef, axis, backward):
    length = logdec.shape[axis]
    cumulative = lax.cumsum(logdec, axis=axis, reverse=backward)
    whole = jnp.sum(logdec, axis=axis)
    later = lax.broadcasted_iota(jnp.int32, (length, length), 0)
    earlier = lax.broadcasted_iota(jnp.int32, (length, length), 1)
    if backward:
        causal = later <= earlier
    else:
        causal = later >= earlier
    if axis == 1:
        spread = cumulative[:, :, None, :] - cumulative[:, None, :, :]
        within = causal[None, :, :, None]
        mixing = (
            jnp.where(within, jnp.exp(jnp.where(within, spread, 0.0)), 0.0) * outcoef[:, :, None, :]
        )
        local_out = jnp.einsum("ltsh,lshp->lthp", mixing, weighted, precision=lax.Precision.HIGH)
        tail = jnp.exp(whole[:, None, :] - cumulative)
        end_state = jnp.einsum("lsh,lshp->lhp", tail, weighted, precision=lax.Precision.HIGH)
    else:
        spread = cumulative[:, None] - cumulative[None, :]
        within = causal[:, :, None, None]
        mixing = jnp.where(within, jnp.exp(jnp.where(within, spread, 0.0)), 0.0) * outcoef[:, None]
        local_out = jnp.einsum("tslh,slhp->tlhp", mixing, weighted, precision=lax.Precision.HIGH)
        tail = jnp.exp(whole[None] - cumulative)
        end_state = jnp.einsum("slh,slhp->lhp", tail, weighted, precision=lax.Precision.HIGH)
    return (local_out, jnp.exp(whole), end_state, jnp.exp(cumulative) * outcoef)


def relay_chain(decay_end, end_state, count, neighbor):
    factor = decay_end[..., None]

    def relay_turn(number, state_pair):
        running, arrived = state_pair
        arrived = neighbor(running)
        return (end_state + factor * arrived, arrived)

    _, arrived = lax.fori_loop(0, count - 1, relay_turn, (end_state, jnp.zeros_like(end_state)))
    return arrived


def carry_in(decay_end, end_state, direction):
    if direction == 0:
        neighbor = lambda value: passed_along(value, "cols", 1)
        count = lax.axis_size("cols")
    elif direction == 1:
        neighbor = lambda value: passed_along(value, "cols", -1)
        count = lax.axis_size("cols")
    elif direction == 2:
        neighbor = lambda value: passed_along(value, "rows", 1)
        count = lax.axis_size("rows")
    else:
        neighbor = lambda value: passed_along(value, "rows", -1)
        count = lax.axis_size("rows")
    return relay_chain(decay_end, end_state, count, neighbor)


def local(xin, gate_in, w_proj, rate, skip, norm_gain, w_out):
    row_count, col_count, width = xin.shape
    heads = rate.shape[1]
    head = width // heads
    half = heads // 2
    flat = xin.reshape(row_count * col_count, width)
    proj = jnp.dot(flat, w_proj, preferred_element_type=jnp.float32).reshape(
        row_count, col_count, -1
    )
    total = skip * xin.astype(jnp.float32)
    head_view = xin.reshape(row_count, col_count, heads, head)
    for direction in range(4):
        base = direction * 2 * heads
        step_size = jax.nn.softplus(proj[..., base : base + heads])
        input_coef = jnp.repeat(proj[..., base + heads : base + heads + half], 2, axis=-1)
        output_coef = jnp.repeat(proj[..., base + heads + half : base + 2 * heads], 2, axis=-1)
        logdec = -step_size * rate[direction]
        weighted = head_view * (step_size * input_coef)[..., None]
        axis = 1 if direction < 2 else 0
        local_out, decay_end, end_state, reach = line_scan(
            weighted, logdec, output_coef, axis, direction % 2 == 1
        )
        arrived = carry_in(decay_end, end_state, direction)
        if axis == 1:
            local_out = local_out + reach[..., None] * arrived[:, None]
        else:
            local_out = local_out + reach[..., None] * arrived[None]
        total = total + local_out.reshape(row_count, col_count, width)
    scale = lax.rsqrt(jnp.mean(total * total, axis=-1, keepdims=True) + 1e-05)
    normed = (total * scale * norm_gain * jax.nn.silu(gate_in.astype(jnp.float32))).astype(
        jnp.bfloat16
    )
    mixed = jnp.dot(normed.reshape(-1, width), w_out, preferred_element_type=jnp.float32)
    return mixed.reshape(row_count, col_count, -1).astype(jnp.bfloat16)


def solution(mesh):
    in_specs = (P("rows", "cols", None), P("rows", "cols", None), P(), P(), P(), P(), P())
    out_specs = P("rows", "cols", None)
    return jax.shard_map(local, mesh=mesh, in_specs=in_specs, out_specs=out_specs, check_vma=False)
```

profile of v0, /device:TPU:136, one launch (start us, length us, event | category | flops | bytes accessed | tf_op | source)
XLA Modules:
  0.0 1362.2 jit_solution(15384258639860828688)
XLA Ops:
  22.8 550.1 %while.51 = (s32[]{:T(128)}, f32[64,16,64]{2,1,0:T(8,128)}, f32[64,16,64]{2,1,0:T(8,128)}, f32[64,16,1]{1,0,2:T(8,128)S(1)}, f32[64,16,64]{2,1,0:T(8,128)S(1)}, /*index=5*/s32[]{:T(128)}) while((s32[]{:T(128)}, f32[64,16,64]{2,1,0:T(8,128)}, f32[64,16,64]{2,1,0:T(8,128)}, f32[64,16,1]{1,0,2:T(8,128)S(1)}, f32[64,16,64]{2,1,0:T(8,128)S(1)}, ...), condition=%wide.region_15.16_spmd, body=%wide.region_14.15_spmd.sunk | while | flops 131074 | bytes 2887817 | solution.py:50
  26.0 12.6 collective-permute-done.3
  82.5 12.6 collective-permute-done.3
  104.1 9.4 collective-permute-done.3
  154.6 12.6 collective-permute-done.3
  176.2 11.0 collective-permute-done.3
  228.3 12.6 collective-permute-done.3
  249.9 11.0 collective-permute-done.3
  302.1 12.6 collective-permute-done.3
  323.7 11.0 collective-permute-done.3
  401.1 13.4 collective-permute-start.3
  414.5 12.5 collective-permute-done.3
  577.1 11.1 bitcast_add_fusion
  608.5 558.8 %while.50 = (s32[]{:T(128)}, f32[64,16,64]{2,1,0:T(8,128)}, f32[64,16,64]{2,1,0:T(8,128)}, f32[64,16,1]{1,0,2:T(8,128)S(1)}, f32[64,16,64]{2,1,0:T(8,128)S(1)}, /*index=5*/s32[]{:T(128)}) while((s32[]{:T(128)}, f32[64,16,64]{2,1,0:T(8,128)}, f32[64,16,64]{2,1,0:T(8,128)}, f32[64,16,1]{1,0,2:T(8,128)S(1)}, f32[64,16,64]{2,1,0:T(8,128)S(1)}, ...), condition=%wide.region_11.12_spmd, body=%wide.region_10.11_spmd.sunk | while | flops 131074 | bytes 2887817 | solution.py:50
  610.6 17.7 %collective-permute-done.2 = f32[64,16,64]{2,1,0:T(8,128)S(1)} collective-permute-done((f32[64,16,64]{2,1,0:T(8,128)}, f32[64,16,64]{2,1,0:T(8,128)S(1)}, u32[]{:S(2)}, u32[]{:S(2)}) %collective-permute-start.2) | collective-permute-done | bytes 262176 | tf_op jit(solution)/shard_map/while/body/eval_jaxpr/ppermute | solution.py:10
  631.2 13.0 collective-permute-done.2
  647.1 13.0 collective-permute-done.2
  663.0 13.0 collective-permute-done.2
  679.0 13.0 collective-permute-done.2
  694.9 18.7 %collective-permute-done.2 = f32[64,16,64]{2,1,0:T(8,128)S(1)} collective-permute-done((f32[64,16,64]{2,1,0:T(8,128)}, f32[64,16,64]{2,1,0:T(8,128)S(1)}, u32[]{:S(2)}, u32[]{:S(2)}) %collective-permute-start.2) | collective-permute-done | bytes 262176 | tf_op jit(solution)/shard_map/while/body/eval_jaxpr/ppermute | solution.py:10
  716.5 17.7 %collective-permute-done.2 = f32[64,16,64]{2,1,0:T(8,128)S(1)} collective-permute-done((f32[64,16,64]{2,1,0:T(8,128)}, f32[64,16,64]{2,1,0:T(8,128)S(1)}, u32[]{:S(2)}, u32[]{:S(2)}) %collective-permute-start.2) | collective-permute-done | bytes 262176 | tf_op jit(solution)/shard_map/while/body/eval_jaxpr/ppermute | solution.py:10
  737.1 13.1 collective-permute-done.2
  753.1 13.0 collective-permute-done.2
  769.0 17.4 %collective-permute-done.2 = f32[64,16,64]{2,1,0:T(8,128)S(1)} collective-permute-done((f32[64,16,64]{2,1,0:T(8,128)}, f32[64,16,64]{2,1,0:T(8,128)S(1)}, u32[]{:S(2)}, u32[]{:S(2)}) %collective-permute-start.2) | collective-permute-done | bytes 262176 | tf_op jit(solution)/shard_map/while/body/eval_jaxpr/ppermute | solution.py:10
  789.4 17.3 %collective-permute-done.2 = f32[64,16,64]{2,1,0:T(8,128)S(1)} collective-permute-done((f32[64,16,64]{2,1,0:T(8,128)}, f32[64,16,64]{2,1,0:T(8,128)S(1)}, u32[]{:S(2)}, u32[]{:S(2)}) %collective-permute-start.2) | collective-permute-done | bytes 262176 | tf_op jit(solution)/shard_map/while/body/eval_jaxpr/ppermute | solution.py:10
  809.6 14.7 %collective-permute-done.2 = f32[64,16,64]{2,1,0:T(8,128)S(1)} collective-permute-done((f32[64,16,64]{2,1,0:T(8,128)}, f32[64,16,64]{2,1,0:T(8,128)S(1)}, u32[]{:S(2)}, u32[]{:S(2)}) %collective-permute-start.2) | collective-permute-done | bytes 262176 | tf_op jit(solution)/shard_map/while/body/eval_jaxpr/ppermute | solution.py:10
  827.1 13.0 collective-permute-done.2
  843.0 17.4 %collective-permute-done.2 = f32[64,16,64]{2,1,0:T(8,128)S(1)} collective-permute-done((f32[64,16,64]{2,1,0:T(8,128)}, f32[64,16,64]{2,1,0:T(8,128)S(1)}, u32[]{:S(2)}, u32[]{:S(2)}) %collective-permute-start.2) | collective-permute-done | bytes 262176 | tf_op jit(solution)/shard_map/while/body/eval_jaxpr/ppermute | solution.py:10
  863.4 17.3 %collective-permute-done.2 = f32[64,16,64]{2,1,0:T(8,128)S(1)} collective-permute-done((f32[64,16,64]{2,1,0:T(8,128)}, f32[64,16,64]{2,1,0:T(8,128)S(1)}, u32[]{:S(2)}, u32[]{:S(2)}) %collective-permute-start.2) | collective-permute-done | bytes 262176 | tf_op jit(solution)/shard_map/while/body/eval_jaxpr/ppermute | solution.py:10
  883.6 14.6 %collective-permute-done.2 = f32[64,16,64]{2,1,0:T(8,128)S(1)} collective-permute-done((f32[64,16,64]{2,1,0:T(8,128)}, f32[64,16,64]{2,1,0:T(8,128)S(1)}, u32[]{:S(2)}, u32[]{:S(2)}) %collective-permute-start.2) | collective-permute-done | bytes 262176 | tf_op jit(solution)/shard_map/while/body/eval_jaxpr/ppermute | solution.py:10
  901.1 13.0 collective-permute-done.2
  917.0 17.4 %collective-permute-done.2 = f32[64,16,64]{2,1,0:T(8,128)S(1)} collective-permute-done((f32[64,16,64]{2,1,0:T(8,128)}, f32[64,16,64]{2,1,0:T(8,128)S(1)}, u32[]{:S(2)}, u32[]{:S(2)}) %collective-permute-start.2) | collective-permute-done | bytes 262176 | tf_op jit(solution)/shard_map/while/body/eval_jaxpr/ppermute | solution.py:10
  937.4 17.3 %collective-permute-done.2 = f32[64,16,64]{2,1,0:T(8,128)S(1)} collective-permute-done((f32[64,16,64]{2,1,0:T(8,128)}, f32[64,16,64]{2,1,0:T(8,128)S(1)}, u32[]{:S(2)}, u32[]{:S(2)}) %collective-permute-start.2) | collective-permute-done | bytes 262176 | tf_op jit(solution)/shard_map/while/body/eval_jaxpr/ppermute | solution.py:10
  957.6 14.6 %collective-permute-done.2 = f32[64,16,64]{2,1,0:T(8,128)S(1)} collective-permute-done((f32[64,16,64]{2,1,0:T(8,128)}, f32[64,16,64]{2,1,0:T(8,128)S(1)}, u32[]{:S(2)}, u32[]{:S(2)}) %collective-permute-start.2) | collective-permute-done | bytes 262176 | tf_op jit(solution)/shard_map/while/body/eval_jaxpr/ppermute | solution.py:10
  975.1 13.0 collective-permute-done.2
  991.0 17.5 %collective-permute-done.2 = f32[64,16,64]{2,1,0:T(8,128)S(1)} collective-permute-done((f32[64,16,64]{2,1,0:T(8,128)}, f32[64,16,64]{2,1,0:T(8,128)S(1)}, u32[]{:S(2)}, u32[]{:S(2)}) %collective-permute-start.2) | collective-permute-done | bytes 262176 | tf_op jit(solution)/shard_map/while/body/eval_jaxpr/ppermute | solution.py:10
  1011.4 17.3 %collective-permute-done.2 = f32[64,16,64]{2,1,0:T(8,128)S(1)} collective-permute-done((f32[64,16,64]{2,1,0:T(8,128)}, f32[64,16,64]{2,1,0:T(8,128)S(1)}, u32[]{:S(2)}, u32[]{:S(2)}) %collective-permute-start.2) | collective-permute-done | bytes 262176 | tf_op jit(solution)/shard_map/while/body/eval_jaxpr/ppermute | solution.py:10
  1031.6 14.5 %collective-permute-done.2 = f32[64,16,64]{2,1,0:T(8,128)S(1)} collective-permute-done((f32[64,16,64]{2,1,0:T(8,128)}, f32[64,16,64]{2,1,0:T(8,128)S(1)}, u32[]{:S(2)}, u32[]{:S(2)}) %collective-permute-start.2) | collective-permute-done | bytes 262176 | tf_op jit(solution)/shard_map/while/body/eval_jaxpr/ppermute | solution.py:10
  1049.0 13.0 collective-permute-done.2
  1065.0 17.5 %collective-permute-done.2 = f32[64,16,64]{2,1,0:T(8,128)S(1)} collective-permute-done((f32[64,16,64]{2,1,0:T(8,128)}, f32[64,16,64]{2,1,0:T(8,128)S(1)}, u32[]{:S(2)}, u32[]{:S(2)}) %collective-permute-start.2) | collective-permute-done | bytes 262176 | tf_op jit(solution)/shard_map/while/body/eval_jaxpr/ppermute | solution.py:10
  1085.4 17.3 %collective-permute-done.2 = f32[64,16,64]{2,1,0:T(8,128)S(1)} collective-permute-done((f32[64,16,64]{2,1,0:T(8,128)}, f32[64,16,64]{2,1,0:T(8,128)S(1)}, u32[]{:S(2)}, u32[]{:S(2)}) %collective-permute-start.2) | collective-permute-done | bytes 262176 | tf_op jit(solution)/shard_map/while/body/eval_jaxpr/ppermute | solution.py:10
  1105.6 13.0 collective-permute-done.2
  1121.5 13.0 collective-permute-done.2
  1137.5 13.0 collective-permute-done.2
  1153.4 13.0 collective-permute-done.2
  1170.7 11.1 bitcast_add_fusion.1
  1213.0 51.3 %while.49 = (s32[]{:T(128)}, f32[8,16,64]{2,1,0:T(8,128)S(1)}, f32[8,16,64]{2,1,0:T(8,128)}, f32[8,16,1]{1,0,2:T(8,128)S(1)}, f32[8,16,64]{2,1,0:T(8,128)S(1)}, /*index=5*/s32[]{:T(128)}) while((s32[]{:T(128)}, f32[8,16,64]{2,1,0:T(8,128)S(1)}, f32[8,16,64]{2,1,0:T(8,128)}, f32[8,16,1]{1,0,2:T(8,128)S(1)}, f32[8,16,64]{2,1,0:T(8,128)S(1)}, ...), condition=%wide.region_7.8_spmd, body=%wide.region_6.7_spmd.sunk | while | flops 16386 | bytes 361097 | solution.py:50
  1289.8 54.2 %while.48 = (s32[]{:T(128)}, f32[8,16,64]{2,1,0:T(8,128)S(1)}, f32[8,16,64]{2,1,0:T(8,128)}, f32[8,16,1]{1,0,2:T(8,128)S(1)}, f32[8,16,64]{2,1,0:T(8,128)S(1)}, /*index=5*/s32[]{:T(128)}) while((s32[]{:T(128)}, f32[8,16,64]{2,1,0:T(8,128)S(1)}, f32[8,16,64]{2,1,0:T(8,128)}, f32[8,16,1]{1,0,2:T(8,128)S(1)}, f32[8,16,64]{2,1,0:T(8,128)S(1)}, ...), condition=%wide.region_3.4_spmd, body=%wide.region_2.3_spmd.sunk | while | flops 16386 | bytes 361097 | solution.py:50
  (465 shorter events, 739.1 us)
Async XLA Ops:
  22.8 15.8 %collective-permute-start.3 = (f32[64,16,64]{2,1,0:T(8,128)}, f32[64,16,64]{2,1,0:T(8,128)S(1)}, u32[]{:S(2)}, u32[]{:S(2)}) collective-permute-start(f32[64,16,64]{2,1,0:T(8,128)} %get-tuple-element.327), channel_id=1, source_target_pairs={{8,0},{16,8},{24,16},{32,24},{40,32},{48,40},{56,48},{64,56},{72,6... | collective-permute-start | bytes 786440 | tf_op jit(solution)/shard_map/while/body/eval_jaxpr/ppermute | solution.py:10
  39.6 16.9 %collective-permute-start.3 = (f32[64,16,64]{2,1,0:T(8,128)}, f32[64,16,64]{2,1,0:T(8,128)S(1)}, u32[]{:S(2)}, u32[]{:S(2)}) collective-permute-start(f32[64,16,64]{2,1,0:T(8,128)} %get-tuple-element.327), channel_id=1, source_target_pairs={{8,0},{16,8},{24,16},{32,24},{40,32},{48,40},{56,48},{64,56},{72,6... | collective-permute-start | bytes 786440 | tf_op jit(solution)/shard_map/while/body/eval_jaxpr/ppermute | solution.py:10
  57.5 16.0 %collective-permute-start.3 = (f32[64,16,64]{2,1,0:T(8,128)}, f32[64,16,64]{2,1,0:T(8,128)S(1)}, u32[]{:S(2)}, u32[]{:S(2)}) collective-permute-start(f32[64,16,64]{2,1,0:T(8,128)} %get-tuple-element.327), channel_id=1, source_target_pairs={{8,0},{16,8},{24,16},{32,24},{40,32},{48,40},{56,48},{64,56},{72,6... | collective-permute-start | bytes 786440 | tf_op jit(solution)/shard_map/while/body/eval_jaxpr/ppermute | solution.py:10
  74.5 20.6 %collective-permute-start.3 = (f32[64,16,64]{2,1,0:T(8,128)}, f32[64,16,64]{2,1,0:T(8,128)S(1)}, u32[]{:S(2)}, u32[]{:S(2)}) collective-permute-start(f32[64,16,64]{2,1,0:T(8,128)} %get-tuple-element.327), channel_id=1, source_target_pairs={{8,0},{16,8},{24,16},{32,24},{40,32},{48,40},{56,48},{64,56},{72,6... | collective-permute-start | bytes 786440 | tf_op jit(solution)/shard_map/while/body/eval_jaxpr/ppermute | solution.py:10
  96.1 17.4 %collective-permute-start.3 = (f32[64,16,64]{2,1,0:T(8,128)}, f32[64,16,64]{2,1,0:T(8,128)S(1)}, u32[]{:S(2)}, u32[]{:S(2)}) collective-permute-start(f32[64,16,64]{2,1,0:T(8,128)} %get-tuple-element.327), channel_id=1, source_target_pairs={{8,0},{16,8},{24,16},{32,24},{40,32},{48,40},{56,48},{64,56},{72,6... | collective-permute-start | bytes 786440 | tf_op jit(solution)/shard_map/while/body/eval_jaxpr/ppermute | solution.py:10
  114.5 15.0 %collective-permute-start.3 = (f32[64,16,64]{2,1,0:T(8,128)}, f32[64,16,64]{2,1,0:T(8,128)S(1)}, u32[]{:S(2)}, u32[]{:S(2)}) collective-permute-start(f32[64,16,64]{2,1,0:T(8,128)} %get-tuple-element.327), channel_id=1, source_target_pairs={{8,0},{16,8},{24,16},{32,24},{40,32},{48,40},{56,48},{64,56},{72,6... | collective-permute-start | bytes 786440 | tf_op jit(solution)/shard_map/while/body/eval_jaxpr/ppermute | solution.py:10
  130.5 15.0 %collective-permute-start.3 = (f32[64,16,64]{2,1,0:T(8,128)}, f32[64,16,64]{2,1,0:T(8,128)S(1)}, u32[]{:S(2)}, u32[]{:S(2)}) collective-permute-start(f32[64,16,64]{2,1,0:T(8,128)} %get-tuple-element.327), channel_id=1, source_target_pairs={{8,0},{16,8},{24,16},{32,24},{40,32},{48,40},{56,48},{64,56},{72,6... | collective-permute-start | bytes 786440 | tf_op jit(solution)/shard_map/while/body/eval_jaxpr/ppermute | solution.py:10
  146.5 20.6 %collective-permute-start.3 = (f32[64,16,64]{2,1,0:T(8,128)}, f32[64,16,64]{2,1,0:T(8,128)S(1)}, u32[]{:S(2)}, u32[]{:S(2)}) collective-permute-start(f32[64,16,64]{2,1,0:T(8,128)} %get-tuple-element.327), channel_id=1, source_target_pairs={{8,0},{16,8},{24,16},{32,24},{40,32},{48,40},{56,48},{64,56},{72,6... | collective-permute-start | bytes 786440 | tf_op jit(solution)/shard_map/while/body/eval_jaxpr/ppermute | solution.py:10
  168.2 19.1 %collective-permute-start.3 = (f32[64,16,64]{2,1,0:T(8,128)}, f32[64,16,64]{2,1,0:T(8,128)S(1)}, u32[]{:S(2)}, u32[]{:S(2)}) collective-permute-start(f32[64,16,64]{2,1,0:T(8,128)} %get-tuple-element.327), channel_id=1, source_target_pairs={{8,0},{16,8},{24,16},{32,24},{40,32},{48,40},{56,48},{64,56},{72,6... | collective-permute-start | bytes 786440 | tf_op jit(solution)/shard_map/while/body/eval_jaxpr/ppermute | solution.py:10
  188.2 15.0 %collective-permute-start.3 = (f32[64,16,64]{2,1,0:T(8,128)}, f32[64,16,64]{2,1,0:T(8,128)S(1)}, u32[]{:S(2)}, u32[]{:S(2)}) collective-permute-start(f32[64,16,64]{2,1,0:T(8,128)} %get-tuple-element.327), channel_id=1, source_target_pairs={{8,0},{16,8},{24,16},{32,24},{40,32},{48,40},{56,48},{64,56},{72,6... | collective-permute-start | bytes 786440 | tf_op jit(solution)/shard_map/while/body/eval_jaxpr/ppermute | solution.py:10
  204.3 15.0 %collective-permute-start.3 = (f32[64,16,64]{2,1,0:T(8,128)}, f32[64,16,64]{2,1,0:T(8,128)S(1)}, u32[]{:S(2)}, u32[]{:S(2)}) collective-permute-start(f32[64,16,64]{2,1,0:T(8,128)} %get-tuple-element.327), channel_id=1, source_target_pairs={{8,0},{16,8},{24,16},{32,24},{40,32},{48,40},{56,48},{64,56},{72,6... | collective-permute-start | bytes 786440 | tf_op jit(solution)/shard_map/while/body/eval_jaxpr/ppermute | solution.py:10
  220.3 20.6 %collective-permute-start.3 = (f32[64,16,64]{2,1,0:T(8,128)}, f32[64,16,64]{2,1,0:T(8,128)S(1)}, u32[]{:S(2)}, u32[]{:S(2)}) collective-permute-start(f32[64,16,64]{2,1,0:T(8,128)} %get-tuple-element.327), channel_id=1, source_target_pairs={{8,0},{16,8},{24,16},{32,24},{40,32},{48,40},{56,48},{64,56},{72,6... | collective-permute-start | bytes 786440 | tf_op jit(solution)/shard_map/while/body/eval_jaxpr/ppermute | solution.py:10
  241.9 19.1 %collective-permute-start.3 = (f32[64,16,64]{2,1,0:T(8,128)}, f32[64,16,64]{2,1,0:T(8,128)S(1)}, u32[]{:S(2)}, u32[]{:S(2)}) collective-permute-start(f32[64,16,64]{2,1,0:T(8,128)} %get-tuple-element.327), channel_id=1, source_target_pairs={{8,0},{16,8},{24,16},{32,24},{40,32},{48,40},{56,48},{64,56},{72,6... | collective-permute-start | bytes 786440 | tf_op jit(solution)/shard_map/while/body/eval_jaxpr/ppermute | solution.py:10
  262.0 15.0 %collective-permute-start.3 = (f32[64,16,64]{2,1,0:T(8,128)}, f32[64,16,64]{2,1,0:T(8,128)S(1)}, u32[]{:S(2)}, u32[]{:S(2)}) collective-permute-start(f32[64,16,64]{2,1,0:T(8,128)} %get-tuple-element.327), channel_id=1, source_target_pairs={{8,0},{16,8},{24,16},{32,24},{40,32},{48,40},{56,48},{64,56},{72,6... | collective-permute-start | bytes 786440 | tf_op jit(solution)/shard_map/while/body/eval_jaxpr/ppermute | solution.py:10
  278.0 15.0 %collective-permute-start.3 = (f32[64,16,64]{2,1,0:T(8,128)}, f32[64,16,64]{2,1,0:T(8,128)S(1)}, u32[]{:S(2)}, u32[]{:S(2)}) collective-permute-start(f32[64,16,64]{2,1,0:T(8,128)} %get-tuple-element.327), channel_id=1, source_target_pairs={{8,0},{16,8},{24,16},{32,24},{40,32},{48,40},{56,48},{64,56},{72,6... | collective-permute-start | bytes 786440 | tf_op jit(solution)/shard_map/while/body/eval_jaxpr/ppermute | solution.py:10
  294.0 20.6 %collective-permute-start.3 = (f32[64,16,64]{2,1,0:T(8,128)}, f32[64,16,64]{2,1,0:T(8,128)S(1)}, u32[]{:S(2)}, u32[]{:S(2)}) collective-permute-start(f32[64,16,64]{2,1,0:T(8,128)} %get-tuple-element.327), channel_id=1, source_target_pairs={{8,0},{16,8},{24,16},{32,24},{40,32},{48,40},{56,48},{64,56},{72,6... | collective-permute-start | bytes 786440 | tf_op jit(solution)/shard_map/while/body/eval_jaxpr/ppermute | solution.py:10
  315.7 19.1 %collective-permute-start.3 = (f32[64,16,64]{2,1,0:T(8,128)}, f32[64,16,64]{2,1,0:T(8,128)S(1)}, u32[]{:S(2)}, u32[]{:S(2)}) collective-permute-start(f32[64,16,64]{2,1,0:T(8,128)} %get-tuple-element.327), channel_id=1, source_target_pairs={{8,0},{16,8},{24,16},{32,24},{40,32},{48,40},{56,48},{64,56},{72,6... | collective-permute-start | bytes 786440 | tf_op jit(solution)/shard_map/while/body/eval_jaxpr/ppermute | solution.py:10
  335.7 15.0 %collective-permute-start.3 = (f32[64,16,64]{2,1,0:T(8,128)}, f32[64,16,64]{2,1,0:T(8,128)S(1)}, u32[]{:S(2)}, u32[]{:S(2)}) collective-permute-start(f32[64,16,64]{2,1,0:T(8,128)} %get-tuple-element.327), channel_id=1, source_target_pairs={{8,0},{16,8},{24,16},{32,24},{40,32},{48,40},{56,48},{64,56},{72,6... | collective-permute-start | bytes 786440 | tf_op jit(solution)/shard_map/while/body/eval_jaxpr/ppermute | solution.py:10
  351.7 15.0 %collective-permute-start.3 = (f32[64,16,64]{2,1,0:T(8,128)}, f32[64,16,64]{2,1,0:T(8,128)S(1)}, u32[]{:S(2)}, u32[]{:S(2)}) collective-permute-start(f32[64,16,64]{2,1,0:T(8,128)} %get-tuple-element.327), channel_id=1, source_target_pairs={{8,0},{16,8},{24,16},{32,24},{40,32},{48,40},{56,48},{64,56},{72,6... | collective-permute-start | bytes 786440 | tf_op jit(solution)/shard_map/while/body/eval_jaxpr/ppermute | solution.py:10
  367.8 16.3 %collective-permute-start.3 = (f32[64,16,64]{2,1,0:T(8,128)}, f32[64,16,64]{2,1,0:T(8,128)S(1)}, u32[]{:S(2)}, u32[]{:S(2)}) collective-permute-start(f32[64,16,64]{2,1,0:T(8,128)} %get-tuple-element.327), channel_id=1, source_target_pairs={{8,0},{16,8},{24,16},{32,24},{40,32},{48,40},{56,48},{64,56},{72,6... | collective-permute-start | bytes 786440 | tf_op jit(solution)/shard_map/while/body/eval_jaxpr/ppermute | solution.py:10
  385.0 15.1 %collective-permute-start.3 = (f32[64,16,64]{2,1,0:T(8,128)}, f32[64,16,64]{2,1,0:T(8,128)S(1)}, u32[]{:S(2)}, u32[]{:S(2)}) collective-permute-start(f32[64,16,64]{2,1,0:T(8,128)} %get-tuple-element.327), channel_id=1, source_target_pairs={{8,0},{16,8},{24,16},{32,24},{40,32},{48,40},{56,48},{64,56},{72,6... | collective-permute-start | bytes 786440 | tf_op jit(solution)/shard_map/while/body/eval_jaxpr/ppermute | solution.py:10
  401.1 25.9 %collective-permute-start.3 = (f32[64,16,64]{2,1,0:T(8,128)}, f32[64,16,64]{2,1,0:T(8,128)S(1)}, u32[]{:S(2)}, u32[]{:S(2)}) collective-permute-start(f32[64,16,64]{2,1,0:T(8,128)} %get-tuple-element.327), channel_id=1, source_target_pairs={{8,0},{16,8},{24,16},{32,24},{40,32},{48,40},{56,48},{64,56},{72,6... | collective-permute-start | bytes 786440 | tf_op jit(solution)/shard_map/while/body/eval_jaxpr/ppermute | solution.py:10
  428.0 15.0 %collective-permute-start.3 = (f32[64,16,64]{2,1,0:T(8,128)}, f32[64,16,64]{2,1,0:T(8,128)S(1)}, u32[]{:S(2)}, u32[]{:S(2)}) collective-permute-start(f32[64,16,64]{2,1,0:T(8,128)} %get-tuple-element.327), channel_id=1, source_target_pairs={{8,0},{16,8},{24,16},{32,24},{40,32},{48,40},{56,48},{64,56},{72,6... | collective-permute-start | bytes 786440 | tf_op jit(solution)/shard_map/while/body/eval_jaxpr/ppermute | solution.py:10
  460.0 16.0 %collective-permute-start.3 = (f32[64,16,64]{2,1,0:T(8,128)}, f32[64,16,64]{2,1,0:T(8,128)S(1)}, u32[]{:S(2)}, u32[]{:S(2)}) collective-permute-start(f32[64,16,64]{2,1,0:T(8,128)} %get-tuple-element.327), channel_id=1, source_target_pairs={{8,0},{16,8},{24,16},{32,24},{40,32},{48,40},{56,48},{64,56},{72,6... | collective-permute-start | bytes 786440 | tf_op jit(solution)/shard_map/while/body/eval_jaxpr/ppermute | solution.py:10
  477.0 15.0 %collective-permute-start.3 = (f32[64,16,64]{2,1,0:T(8,128)}, f32[64,16,64]{2,1,0:T(8,128)S(1)}, u32[]{:S(2)}, u32[]{:S(2)}) collective-permute-start(f32[64,16,64]{2,1,0:T(8,128)} %get-tuple-element.327), channel_id=1, source_target_pairs={{8,0},{16,8},{24,16},{32,24},{40,32},{48,40},{56,48},{64,56},{72,6... | collective-permute-start | bytes 786440 | tf_op jit(solution)/shard_map/while/body/eval_jaxpr/ppermute | solution.py:10
  493.0 15.0 %collective-permute-start.3 = (f32[64,16,64]{2,1,0:T(8,128)}, f32[64,16,64]{2,1,0:T(8,128)S(1)}, u32[]{:S(2)}, u32[]{:S(2)}) collective-permute-start(f32[64,16,64]{2,1,0:T(8,128)} %get-tuple-element.327), channel_id=1, source_target_pairs={{8,0},{16,8},{24,16},{32,24},{40,32},{48,40},{56,48},{64,56},{72,6... | collective-permute-start | bytes 786440 | tf_op jit(solution)/shard_map/while/body/eval_jaxpr/ppermute | solution.py:10
  509.0 15.0 %collective-permute-start.3 = (f32[64,16,64]{2,1,0:T(8,128)}, f32[64,16,64]{2,1,0:T(8,128)S(1)}, u32[]{:S(2)}, u32[]{:S(2)}) collective-permute-start(f32[64,16,64]{2,1,0:T(8,128)} %get-tuple-element.327), channel_id=1, source_target_pairs={{8,0},{16,8},{24,16},{32,24},{40,32},{48,40},{56,48},{64,56},{72,6... | collective-permute-start | bytes 786440 | tf_op jit(solution)/shard_map/while/body/eval_jaxpr/ppermute | solution.py:10
  525.0 15.0 %collective-permute-start.3 = (f32[64,16,64]{2,1,0:T(8,128)}, f32[64,16,64]{2,1,0:T(8,128)S(1)}, u32[]{:S(2)}, u32[]{:S(2)}) collective-permute-start(f32[64,16,64]{2,1,0:T(8,128)} %get-tuple-element.327), channel_id=1, source_target_pairs={{8,0},{16,8},{24,16},{32,24},{40,32},{48,40},{56,48},{64,56},{72,6... | collective-permute-start | bytes 786440 | tf_op jit(solution)/shard_map/while/body/eval_jaxpr/ppermute | solution.py:10
  541.0 15.0 %collective-permute-start.3 = (f32[64,16,64]{2,1,0:T(8,128)}, f32[64,16,64]{2,1,0:T(8,128)S(1)}, u32[]{:S(2)}, u32[]{:S(2)}) collective-permute-start(f32[64,16,64]{2,1,0:T(8,128)} %get-tuple-element.327), channel_id=1, source_target_pairs={{8,0},{16,8},{24,16},{32,24},{40,32},{48,40},{56,48},{64,56},{72,6... | collective-permute-start | bytes 786440 | tf_op jit(solution)/shard_map/while/body/eval_jaxpr/ppermute | solution.py:10
  608.5 19.7 %collective-permute-start.2 = (f32[64,16,64]{2,1,0:T(8,128)}, f32[64,16,64]{2,1,0:T(8,128)S(1)}, u32[]{:S(2)}, u32[]{:S(2)}) collective-permute-start(f32[64,16,64]{2,1,0:T(8,128)} %get-tuple-element.345), channel_id=1, source_target_pairs={{0,8},{8,16},{16,24},{24,32},{32,40},{40,48},{48,56},{56,64},{64,7... | collective-permute-start | bytes 786440 | tf_op jit(solution)/shard_map/while/body/eval_jaxpr/ppermute | solution.py:10
  677.0 14.9 %collective-permute-start.2 = (f32[64,16,64]{2,1,0:T(8,128)}, f32[64,16,64]{2,1,0:T(8,128)S(1)}, u32[]{:S(2)}, u32[]{:S(2)}) collective-permute-start(f32[64,16,64]{2,1,0:T(8,128)} %get-tuple-element.345), channel_id=1, source_target_pairs={{0,8},{8,16},{16,24},{24,32},{32,40},{40,48},{48,56},{56,64},{64,7... | collective-permute-start | bytes 786440 | tf_op jit(solution)/shard_map/while/body/eval_jaxpr/ppermute | solution.py:10
  693.0 20.6 %collective-permute-start.2 = (f32[64,16,64]{2,1,0:T(8,128)}, f32[64,16,64]{2,1,0:T(8,128)S(1)}, u32[]{:S(2)}, u32[]{:S(2)}) collective-permute-start(f32[64,16,64]{2,1,0:T(8,128)} %get-tuple-element.345), channel_id=1, source_target_pairs={{0,8},{8,16},{16,24},{24,32},{32,40},{40,48},{48,56},{56,64},{64,7... | collective-permute-start | bytes 786440 | tf_op jit(solution)/shard_map/while/body/eval_jaxpr/ppermute | solution.py:10
  714.6 19.6 %collective-permute-start.2 = (f32[64,16,64]{2,1,0:T(8,128)}, f32[64,16,64]{2,1,0:T(8,128)S(1)}, u32[]{:S(2)}, u32[]{:S(2)}) collective-permute-start(f32[64,16,64]{2,1,0:T(8,128)} %get-tuple-element.345), channel_id=1, source_target_pairs={{0,8},{8,16},{16,24},{24,32},{32,40},{40,48},{48,56},{56,64},{64,7... | collective-permute-start | bytes 786440 | tf_op jit(solution)/shard_map/while/body/eval_jaxpr/ppermute | solution.py:10
  735.2 15.0 %collective-permute-start.2 = (f32[64,16,64]{2,1,0:T(8,128)}, f32[64,16,64]{2,1,0:T(8,128)S(1)}, u32[]{:S(2)}, u32[]{:S(2)}) collective-permute-start(f32[64,16,64]{2,1,0:T(8,128)} %get-tuple-element.345), channel_id=1, source_target_pairs={{0,8},{8,16},{16,24},{24,32},{32,40},{40,48},{48,56},{56,64},{64,7... | collective-permute-start | bytes 786440 | tf_op jit(solution)/shard_map/while/body/eval_jaxpr/ppermute | solution.py:10
  767.1 19.3 %collective-permute-start.2 = (f32[64,16,64]{2,1,0:T(8,128)}, f32[64,16,64]{2,1,0:T(8,128)S(1)}, u32[]{:S(2)}, u32[]{:S(2)}) collective-permute-start(f32[64,16,64]{2,1,0:T(8,128)} %get-tuple-element.345), channel_id=1, source_target_pairs={{0,8},{8,16},{16,24},{24,32},{32,40},{40,48},{48,56},{56,64},{64,7... | collective-permute-start | bytes 786440 | tf_op jit(solution)/shard_map/while/body/eval_jaxpr/ppermute | solution.py:10
  787.4 19.2 %collective-permute-start.2 = (f32[64,16,64]{2,1,0:T(8,128)}, f32[64,16,64]{2,1,0:T(8,128)S(1)}, u32[]{:S(2)}, u32[]{:S(2)}) collective-permute-start(f32[64,16,64]{2,1,0:T(8,128)} %get-tuple-element.345), channel_id=1, source_target_pairs={{0,8},{8,16},{16,24},{24,32},{32,40},{40,48},{48,56},{56,64},{64,7... | collective-permute-start | bytes 786440 | tf_op jit(solution)/shard_map/while/body/eval_jaxpr/ppermute | solution.py:10
  807.6 16.6 %collective-permute-start.2 = (f32[64,16,64]{2,1,0:T(8,128)}, f32[64,16,64]{2,1,0:T(8,128)S(1)}, u32[]{:S(2)}, u32[]{:S(2)}) collective-permute-start(f32[64,16,64]{2,1,0:T(8,128)} %get-tuple-element.345), channel_id=1, source_target_pairs={{0,8},{8,16},{16,24},{24,32},{32,40},{40,48},{48,56},{56,64},{64,7... | collective-permute-start | bytes 786440 | tf_op jit(solution)/shard_map/while/body/eval_jaxpr/ppermute | solution.py:10
  841.1 19.3 %collective-permute-start.2 = (f32[64,16,64]{2,1,0:T(8,128)}, f32[64,16,64]{2,1,0:T(8,128)S(1)}, u32[]{:S(2)}, u32[]{:S(2)}) collective-permute-start(f32[64,16,64]{2,1,0:T(8,128)} %get-tuple-element.345), channel_id=1, source_target_pairs={{0,8},{8,16},{16,24},{24,32},{32,40},{40,48},{48,56},{56,64},{64,7... | collective-permute-start | bytes 786440 | tf_op jit(solution)/shard_map/while/body/eval_jaxpr/ppermute | solution.py:10
  861.5 19.2 %collective-permute-start.2 = (f32[64,16,64]{2,1,0:T(8,128)}, f32[64,16,64]{2,1,0:T(8,128)S(1)}, u32[]{:S(2)}, u32[]{:S(2)}) collective-permute-start(f32[64,16,64]{2,1,0:T(8,128)} %get-tuple-element.345), channel_id=1, source_target_pairs={{0,8},{8,16},{16,24},{24,32},{32,40},{40,48},{48,56},{56,64},{64,7... | collective-permute-start | bytes 786440 | tf_op jit(solution)/shard_map/while/body/eval_jaxpr/ppermute | solution.py:10
  881.7 16.5 %collective-permute-start.2 = (f32[64,16,64]{2,1,0:T(8,128)}, f32[64,16,64]{2,1,0:T(8,128)S(1)}, u32[]{:S(2)}, u32[]{:S(2)}) collective-permute-start(f32[64,16,64]{2,1,0:T(8,128)} %get-tuple-element.345), channel_id=1, source_target_pairs={{0,8},{8,16},{16,24},{24,32},{32,40},{40,48},{48,56},{56,64},{64,7... | collective-permute-start | bytes 786440 | tf_op jit(solution)/shard_map/while/body/eval_jaxpr/ppermute | solution.py:10
  915.1 19.4 %collective-permute-start.2 = (f32[64,16,64]{2,1,0:T(8,128)}, f32[64,16,64]{2,1,0:T(8,128)S(1)}, u32[]{:S(2)}, u32[]{:S(2)}) collective-permute-start(f32[64,16,64]{2,1,0:T(8,128)} %get-tuple-element.345), channel_id=1, source_target_pairs={{0,8},{8,16},{16,24},{24,32},{32,40},{40,48},{48,56},{56,64},{64,7... | collective-permute-start | bytes 786440 | tf_op jit(solution)/shard_map/while/body/eval_jaxpr/ppermute | solution.py:10
  935.5 19.2 %collective-permute-start.2 = (f32[64,16,64]{2,1,0:T(8,128)}, f32[64,16,64]{2,1,0:T(8,128)S(1)}, u32[]{:S(2)}, u32[]{:S(2)}) collective-permute-start(f32[64,16,64]{2,1,0:T(8,128)} %get-tuple-element.345), channel_id=1, source_target_pairs={{0,8},{8,16},{16,24},{24,32},{32,40},{40,48},{48,56},{56,64},{64,7... | collective-permute-start | bytes 786440 | tf_op jit(solution)/shard_map/while/body/eval_jaxpr/ppermute | solution.py:10
  955.7 16.5 %collective-permute-start.2 = (f32[64,16,64]{2,1,0:T(8,128)}, f32[64,16,64]{2,1,0:T(8,128)S(1)}, u32[]{:S(2)}, u32[]{:S(2)}) collective-permute-start(f32[64,16,64]{2,1,0:T(8,128)} %get-tuple-element.345), channel_id=1, source_target_pairs={{0,8},{8,16},{16,24},{24,32},{32,40},{40,48},{48,56},{56,64},{64,7... | collective-permute-start | bytes 786440 | tf_op jit(solution)/shard_map/while/body/eval_jaxpr/ppermute | solution.py:10
  989.1 19.4 %collective-permute-start.2 = (f32[64,16,64]{2,1,0:T(8,128)}, f32[64,16,64]{2,1,0:T(8,128)S(1)}, u32[]{:S(2)}, u32[]{:S(2)}) collective-permute-start(f32[64,16,64]{2,1,0:T(8,128)} %get-tuple-element.345), channel_id=1, source_target_pairs={{0,8},{8,16},{16,24},{24,32},{32,40},{40,48},{48,56},{56,64},{64,7... | collective-permute-start | bytes 786440 | tf_op jit(solution)/shard_map/while/body/eval_jaxpr/ppermute | solution.py:10
  1009.5 19.2 %collective-permute-start.2 = (f32[64,16,64]{2,1,0:T(8,128)}, f32[64,16,64]{2,1,0:T(8,128)S(1)}, u32[]{:S(2)}, u32[]{:S(2)}) collective-permute-start(f32[64,16,64]{2,1,0:T(8,128)} %get-tuple-element.345), channel_id=1, source_target_pairs={{0,8},{8,16},{16,24},{24,32},{32,40},{40,48},{48,56},{56,64},{64,7... | collective-permute-start | bytes 786440 | tf_op jit(solution)/shard_map/while/body/eval_jaxpr/ppermute | solution.py:10
  1029.7 16.4 %collective-permute-start.2 = (f32[64,16,64]{2,1,0:T(8,128)}, f32[64,16,64]{2,1,0:T(8,128)S(1)}, u32[]{:S(2)}, u32[]{:S(2)}) collective-permute-start(f32[64,16,64]{2,1,0:T(8,128)} %get-tuple-element.345), channel_id=1, source_target_pairs={{0,8},{8,16},{16,24},{24,32},{32,40},{40,48},{48,56},{56,64},{64,7... | collective-permute-start | bytes 786440 | tf_op jit(solution)/shard_map/while/body/eval_jaxpr/ppermute | solution.py:10
  1063.1 19.4 %collective-permute-start.2 = (f32[64,16,64]{2,1,0:T(8,128)}, f32[64,16,64]{2,1,0:T(8,128)S(1)}, u32[]{:S(2)}, u32[]{:S(2)}) collective-permute-start(f32[64,16,64]{2,1,0:T(8,128)} %get-tuple-element.345), channel_id=1, source_target_pairs={{0,8},{8,16},{16,24},{24,32},{32,40},{40,48},{48,56},{56,64},{64,7... | collective-permute-start | bytes 786440 | tf_op jit(solution)/shard_map/while/body/eval_jaxpr/ppermute | solution.py:10
  1083.5 19.2 %collective-permute-start.2 = (f32[64,16,64]{2,1,0:T(8,128)}, f32[64,16,64]{2,1,0:T(8,128)S(1)}, u32[]{:S(2)}, u32[]{:S(2)}) collective-permute-start(f32[64,16,64]{2,1,0:T(8,128)} %get-tuple-element.345), channel_id=1, source_target_pairs={{0,8},{8,16},{16,24},{24,32},{32,40},{40,48},{48,56},{56,64},{64,7... | collective-permute-start | bytes 786440 | tf_op jit(solution)/shard_map/while/body/eval_jaxpr/ppermute | solution.py:10
  (122 other events, 2381.5 us)
where the time goes:
time: 1370 us; the launch traced here: 1360 us
  waiting for transfers between devices  791 us (58%)
  starting transfers between devices  352 us (26%)
  other arithmetic  84.3 us (6%)
  matrix products  69.5 us (5%)
  local copies, waits for them, and re-layouts  64.1 us (5%)
    ppermute x76, waiting for transfers between devices, passed_along(): return lax.ppermute(block, axis, route)  791 us
    ppermute x76, starting transfers between devices, passed_along(): return lax.ppermute(block, axis, route)  352 us
    add x76, other arithmetic, relay_turn(): return (end_state + factor * arrived, arrived)  62.8 us
  transfers between devices with their start and end apart: 76, of which 76 were waited for; matrix products, arithmetic and copies ran while one was open for 0% of the time, Pallas kernels for 0%

commit v1 on v0

v1 whole, which is shorter than its diff:
```python
import functools

import jax
import jax.numpy as jnp
from jax import lax
from jax.experimental import pallas as pl
from jax.experimental.pallas import tpu as pltpu
from jax.sharding import PartitionSpec as P

MESH = pl.DeviceIdType.MESH
F32 = jnp.float32
BF16 = jnp.bfloat16

R, C, E, D, HEADS = 8, 64, 1024, 512, 16
PX = R * C
HALF = C // 2
LANES = 128
TILES = E // LANES
WIDE = E + LANES
NB = 256
CHUNKS = E // NB
ZERO_ROW = 112

NZ, NX, NCORE, NCOL = 4, 4, 2, 8

S_CORE, S_X, S_COLS, S_Z, S_BACK, S_LAST, N_SEM = 0, 1, 4, 11, 14, 17, 18


def split(v):
    hi = v.astype(BF16)
    lo = (v - hi.astype(F32)).astype(BF16)
    return jnp.concatenate([hi, lo], axis=-1)


def mxu(a, b):
    return jnp.dot(a, b, preferred_element_type=F32)


def kernel(x_hbm, g_hbm, wp_hbm, rate_ref, skip_ref, gain_ref, wo_hbm, o_hbm,
           xb, gb, wp, wo, ob, zsel, c1f, v_hl, d_hl, c1_hl, l_hl, h_hl, fv,
           x32, base, ro2, ro3, gg, hd0, hb0, ho0, hd1, hb1, ho1,
           s0, ee, tt, xe, px, gx, tz, ze, sc, rc, fxp, cc, pc, he, hr, nb,
           lsem, ssem, rsem):
    rows = lax.axis_index("rows")
    col = lax.axis_index("cols")
    core = rows % NCORE
    xi = (rows // NCORE) % NX
    zi = rows // (NCORE * NX)

    core_peer = {"rows": rows + 1 - 2 * core}
    x_dst = [(xi + d) % NX for d in range(1, NX)]
    x_peers = [{"rows": (zi * NX + t) * NCORE + core} for t in x_dst]
    z_peers = [{"rows": (((zi + d) % NZ) * NX + xi) * NCORE + core} for d in range(1, NZ)]
    c_peers = [{"cols": (col + d) % NCOL} for d in range(1, NCOL)]
    peers = [core_peer] + x_peers + z_peers + c_peers

    barrier = pltpu.get_barrier_semaphore()
    for peer in peers:
        pl.semaphore_signal(barrier, inc=1, device_id=peer, device_id_type=MESH)

    load_wp = pltpu.make_async_copy(wp_hbm, wp, lsem.at[0])
    load_x = pltpu.make_async_copy(x_hbm, xb, lsem.at[1])
    load_g = pltpu.make_async_copy(g_hbm, gb, lsem.at[2])
    load_wo = pltpu.make_async_copy(wo_hbm, wo, lsem.at[3])
    load_wp.start()
    load_x.start()
    load_g.start()
    load_wo.start()

    def remote(src, dst, number, peer):
        return pltpu.make_async_remote_copy(
            src_ref=src, dst_ref=dst, send_sem=ssem.at[number], recv_sem=rsem.at[number],
            device_id=peer, device_id_type=MESH)

    zsel[...] = jnp.zeros_like(zsel)
    head_row = lax.broadcasted_iota(jnp.int32, (HEADS, E), 0)
    head_col = lax.broadcasted_iota(jnp.int32, (HEADS, E), 1) // (E // HEADS)
    zsel[ZERO_ROW:ZERO_ROW + HEADS, :] = (head_row == head_col).astype(F32).astype(BF16)

    def sel(off, cols):
        part = zsel[ZERO_ROW - off:ZERO_ROW - off + LANES, cols]
        return jnp.concatenate([part, part], axis=0)

    def chunk(n):
        return pl.ds(pl.multiple_of(n * NB, NB), NB)

    def spread(v, off):
        return mxu(split(v), sel(off, slice(0, E)))

    src_lane = lax.broadcasted_iota(jnp.int32, (LANES, 2 * LANES), 0)
    lane = lax.broadcasted_iota(jnp.int32, (LANES, 2 * LANES), 1)
    within = lane % 64
    h = within % 16
    want = 32 * (within // 16) + jnp.where(lane < 128, h, jnp.where(lane < 192, 16 + h // 2, 24 + h // 2))
    pick = (src_lane == want).astype(F32).astype(BF16)
    rate = rate_ref[...]
    rate_lane = jnp.concatenate([rate[k:k + 1, :] for k in range(4)] * 2, axis=1)
    load_wp.wait()
    w2 = mxu(wp[...], pick).astype(BF16)
    load_x.wait()
    proj = mxu(xb[...].reshape(PX, E), w2)
    pre = proj[:, :LANES]
    coef = proj[:, LANES:]
    step = jnp.maximum(pre, 0.0) + jnp.log1p(jnp.exp(-jnp.abs(pre)))
    logd = -rate_lane * step
    lane1 = lax.broadcasted_iota(jnp.int32, (PX, LANES), 1)
    c1 = jnp.where(lane1 < 64, step * coef, coef)
    c1f[...] = c1
    l_hl[...] = split(logd)
    d_hl[...] = split(jnp.exp(logd))
    c1_hl[...] = split(c1)

    logr = [logd[r * C:(r + 1) * C, :] for r in range(R)]
    up = [logr[0]]
    for r in range(1, R):
        up.append(up[-1] + logr[r])
    down = [logr[R - 1]]
    for r in range(R - 2, -1, -1):
        down.insert(0, down[0] + logr[r])
    zero = jnp.zeros((C, LANES), F32)
    lane2 = lax.broadcasted_iota(jnp.int32, (C, LANES), 1)
    falling = (lane2 % 64) >= 48
    for r in range(R):
        before = up[r - 1] if r else zero
        after = down[r + 1] if r < R - 1 else zero
        tail = jnp.where(falling, before, after)
        reach = jnp.where(falling, down[r], up[r])
        v = jnp.exp(jnp.where(lane2 < 64, tail, reach)) * c1[r * C:(r + 1) * C, :]
        v_hl[r] = split(v)
    fv[...] = jnp.exp(up[R - 1])

    def column_ends(start, dst):
        lhs = v_hl[:, pl.ds(start, HALF), :].reshape(R * HALF, 2 * LANES)
        for n in range(CHUNKS):
            cs = slice(n * NB, (n + 1) * NB)
            xh = [xb[r, pl.ds(start, HALF), cs].astype(F32) for r in range(R)]
            for i in range(2):
                w = mxu(lhs, sel(32 + 16 * i, cs))
                acc = w[:HALF] * xh[0]
                for r in range(1, R):
                    acc = acc + w[r * HALF:(r + 1) * HALF] * xh[r]
                dst[i, :, cs] = acc
        for i in range(2):
            dst[i, :, E:] = fv[pl.ds(start, HALF), :]

    own = pl.multiple_of(core * HALF, HALF)
    other = pl.multiple_of((1 - core) * HALF, HALF)
    column_ends(other, s0)
    pl.semaphore_wait(barrier, len(peers))
    to_core = remote(s0, ee.at[core], S_CORE, core_peer)
    to_core.start()
    column_ends(own, ee.at[core])

    to_core.wait_recv()
    for i in range(2):
        first, second = ee.at[i, i], ee.at[1 - i, i]
        t = second[:, :E] + spread(second[:, E:], 32 + 16 * i) * first[:, :E]
        f = second[:, E:] * first[:, E:]
        for q in range(NX):
            tt[q, i, :, :E] = t[q * 8:(q + 1) * 8]
            tt[q, i, :, E:] = f[q * 8:(q + 1) * 8]
    to_x = [remote(tt.at[x_dst[d]], xe.at[xi], S_X + d, x_peers[d]) for d in range(NX - 1)]
    for copy in to_x:
        copy.start()
    xe[xi] = tt[xi]

    bt = lax.broadcasted_iota(jnp.int32, (256, 256), 0)
    bs = lax.broadcasted_iota(jnp.int32, (256, 256), 1)
    same = (bt // C) == (bs // C)
    behind = (same & (bs > bt)).astype(F32).astype(BF16)
    ahead = (same & (bs < bt)).astype(F32).astype(BF16)
    lane3 = lax.broadcasted_iota(jnp.int32, (256, LANES), 1)
    for m in range(PX // 256):
        ps = slice(m * 256, (m + 1) * 256)
        lh = l_hl[ps, :]
        a = mxu(behind, lh)
        b = mxu(ahead, lh)
        cum = jnp.where(lane3 < 16, a[:, :LANES] + a[:, LANES:], b[:, :LANES] + b[:, LANES:])
        h_hl[ps, :] = split(jnp.exp(cum) * c1f[ps, :])
    row_of = lax.broadcasted_iota(jnp.int32, (R, PX), 1) // C
    whole = (row_of == lax.broadcasted_iota(jnp.int32, (R, PX), 0)).astype(F32).astype(BF16)
    ft = mxu(whole, l_hl[...])
    ft = jnp.exp(ft[:, :LANES] + ft[:, LANES:])

    def row_ends(n, _):
        cs = chunk(n)
        for i in range(2):
            w = mxu(h_hl[...], sel(16 * i, cs)).reshape(R, C, NB)
            he[i, :, cs] = jnp.sum(w * xb[:, :, cs].astype(F32), axis=1)
        return 0

    lax.fori_loop(0, CHUNKS, row_ends, 0)
    for i in range(2):
        he[i, :, E:] = ft
    to_cols = [remote(he.at[(col + d) // NCOL], hr.at[col], S_COLS + d - 1, c_peers[d - 1])
               for d in range(1, NCOL)]
    for copy in to_cols:
        copy.start()
    hr[col] = he[0]

    def column_scans(n, _):
        cs = chunk(n)
        xs = [xb[r, :, cs].astype(F32) for r in range(R)]
        sk = skip_ref[:, cs]
        acc = [sk * xs[r] for r in range(R)]
        for r in range(R):
            for t in range(2):
                x32[2 * n + t, r * C:(r + 1) * C, :] = xs[r][:, t * LANES:(t + 1) * LANES]
        for i in range(2):
            off = 32 + 16 * i
            dd = mxu(d_hl[...], sel(off, cs))
            bb = mxu(c1_hl[...], sel(off, cs))
            oo = mxu(c1_hl[...], sel(64 + off, cs))
            state = None
            for r in (range(R) if i == 0 else range(R - 1, -1, -1)):
                ps = slice(r * C, (r + 1) * C)
                push = bb[ps] * xs[r]
                state = push if state is None else dd[ps] * state + push
                acc[r] = acc[r] + oo[ps] * state
        for r in range(R):
            for t in range(2):
                base[2 * n + t, r * C:(r + 1) * C, :] = acc[r][:, t * LANES:(t + 1) * LANES]
        return 0

    lax.fori_loop(0, CHUNKS, column_scans, 0)

    def spread_all(n, _):
        cs = chunk(n)
        dv = d_hl[...]
        cv = c1_hl[...]
        vv = v_hl[...].reshape(PX, 2 * LANES)
        for lhs, off, dst in ((dv, 0, hd0), (cv, 0, hb0), (cv, 64, ho0), (dv, 16, hd1), (cv, 16, hb1),
                              (cv, 80, ho1), (vv, 96, ro2), (vv, 112, ro3)):
            w = mxu(lhs, sel(off, cs))
            for t in range(2):
                dst[2 * n + t] = w[:, t * LANES:(t + 1) * LANES]
        return 0

    lax.fori_loop(0, CHUNKS, spread_all, 0)
    load_g.wait()

    def gates(n, _):
        cs = chunk(n)
        gain = gain_ref[:, cs]
        for r in range(R):
            g = gb[r, :, cs].astype(F32)
            w = gain * (g / (1.0 + jnp.exp(-g)))
            for t in range(2):
                gg[2 * n + t, r * C:(r + 1) * C, :] = w[:, t * LANES:(t + 1) * LANES]
        return 0

    lax.fori_loop(0, CHUNKS, gates, 0)

    for i in range(2):
        fxp[i] = spread(ee[i, i, :, E:], 32 + 16 * i)

    for copy in to_x:
        copy.wait_recv()
    fc = xe[0, 0, :, E:]
    for q in range(1, NX):
        fc = fc * xe[q, 0, :, E:]
    for i in range(2):
        fs = spread(xe[:, i, :, E:].reshape(NX * 8, LANES), 32 + 16 * i)
        acc = jnp.zeros((8, E), F32)
        g = jnp.ones((8, E), F32)
        for q in (range(NX) if i == 0 else range(NX - 1, -1, -1)):
            f = fs[q * 8:(q + 1) * 8]
            px[q, i] = acc
            gx[q, i] = g
            acc = xe[q, i, :, :E] + f * acc
            g = g * f
        tz[i, :, :E] = acc
        tz[i, :, E:] = fc
    to_z = [remote(tz.at[(zi + d) // NZ], ze.at[zi], S_Z + d - 1, z_peers[d - 1]) for d in range(1, NZ)]
    for copy in to_z:
        copy.start()
    ze[zi] = tz[0]

    for copy in to_cols:
        copy.wait_recv()
    fh = hr[:, :, E:].reshape(NCOL * R, LANES)
    f0 = spread(fh, 0)
    f1 = spread(fh, 16)
    in0 = jnp.zeros((R, E), F32)
    in1 = jnp.zeros((R, E), F32)
    for j in range(NCOL):
        in0 = jnp.where(j < col, hr[j, :, :E] + f0[j * R:(j + 1) * R] * in0, in0)
    for j in range(NCOL - 1, -1, -1):
        in1 = jnp.where(j > col, hr[j, :, :E] + f1[j * R:(j + 1) * R] * in1, in1)

    def row_step(c, states):
        out = []
        for at, hd, hb, ho, first in ((c, hd0, hb0, ho0, 0), (C - 1 - c, hd1, hb1, ho1, TILES)):
            ps = pl.ds(at, R, stride=C)
            for t in range(TILES):
                s = hd[t, ps, :] * states[first + t] + hb[t, ps, :] * x32[t, ps, :]
                base[t, ps, :] = base[t, ps, :] + ho[t, ps, :] * s
                out.append(s)
        return tuple(out)

    start = [in0[:, t * LANES:(t + 1) * LANES] for t in range(TILES)]
    start += [in1[:, t * LANES:(t + 1) * LANES] for t in range(TILES)]
    lax.fori_loop(0, C, row_step, tuple(start))
    load_wo.wait()

    for copy in to_z:
        copy.wait_recv()
    fz = ze[:, :, E:].reshape(NZ * 8, LANES)
    for i in range(2):
        fs = spread(fz, 32 + 16 * i)
        acc = jnp.zeros((8, E), F32)
        for j in (range(NZ) if i == 0 else range(NZ - 1, -1, -1)):
            use = (j < zi) if i == 0 else (j > zi)
            acc = jnp.where(use, ze[j, :, :E] + fs[j * 8:(j + 1) * 8] * acc, acc)
        for q in range(NX):
            sc[q, i] = px[q, i] + gx[q, i] * acc
    to_back = [remote(sc.at[x_dst[d]], rc.at[xi], S_BACK + d, x_peers[d]) for d in range(NX - 1)]
    for copy in to_back:
        copy.start()
    rc[xi] = sc[xi]
    for copy in to_back:
        copy.wait_recv()

    for i in range(2):
        for q in range(NX):
            qs = slice(q * 8, (q + 1) * 8)
            carry = rc[q, i]
            cc[i, i, qs, :] = carry
            cc[1 - i, i, qs, :] = ee[i, i, qs, :E] + fxp[i, qs, :] * carry
    to_last = remote(cc.at[1 - core], pc, S_LAST, core_peer)
    to_last.start()

    def finish(start, carry, number):
        def line(r, _):
            ps = pl.ds(pl.multiple_of(r * C + start, HALF), HALF)
            tot = []
            sq = jnp.zeros((HALF, LANES), F32)
            for t in range(TILES):
                ls = slice(t * LANES, (t + 1) * LANES)
                v = base[t, ps, :] + ro2[t, ps, :] * carry[0, :, ls] + ro3[t, ps, :] * carry[1, :, ls]
                sq = sq + v * v
                tot.append(v)
            scale = lax.rsqrt(jnp.sum(sq, axis=-1, keepdims=True) * (1.0 / E) + 1e-05)
            for t in range(TILES):
                ls = slice(t * LANES, (t + 1) * LANES)
                nb[r, :, ls] = (tot[t] * scale * gg[t, ps, :]).astype(BF16)
            return 0

        lax.fori_loop(0, R, line, 0)
        res = mxu(nb[...].reshape(R * HALF, E), wo[...])
        ob[:, pl.ds(start, HALF), :] = res.astype(BF16).reshape(R, HALF, D)
        copy = pltpu.make_async_copy(ob.at[:, pl.ds(start, HALF), :], o_hbm.at[:, pl.ds(start, HALF), :], lsem.at[number])
        copy.start()
        return copy

    out_own = finish(own, cc.at[core], 4)
    to_last.wait_recv()
    out_other = finish(other, pc, 5)
    for copy in [to_core, to_last] + to_x + to_cols + to_z + to_back:
        copy.wait_send()
    out_own.wait()
    out_other.wait()


def local(xin, gate_in, w_proj, rate, skip, norm_gain, w_out):
    vmem = pl.BlockSpec(memory_space=pltpu.VMEM)
    hbm = pl.BlockSpec(memory_space=pl.ANY)
    big = pltpu.VMEM((TILES, PX, LANES), F32)
    compact = pltpu.VMEM((PX, 2 * LANES), BF16)
    scratch = [
        pltpu.VMEM((R, C, E), BF16),
        pltpu.VMEM((R, C, E), BF16),
        pltpu.VMEM((E, LANES), BF16),
        pltpu.VMEM((E, D), BF16),
        pltpu.VMEM((R, C, D), BF16),
        pltpu.VMEM((ZERO_ROW + LANES, E), BF16),
        pltpu.VMEM((PX, LANES), F32),
        pltpu.VMEM((R, C, 2 * LANES), BF16),
        compact, compact, compact, compact,
        pltpu.VMEM((C, LANES), F32),
        big, big, big, big, big, big, big, big, big, big, big,
        pltpu.VMEM((2, HALF, WIDE), F32),
        pltpu.VMEM((2, 2, HALF, WIDE), F32),
        pltpu.VMEM((NX, 2, 8, WIDE), F32),
        pltpu.VMEM((NX, 2, 8, WIDE), F32),
        pltpu.VMEM((NX, 2, 8, E), F32),
        pltpu.VMEM((NX, 2, 8, E), F32),
        pltpu.VMEM((2, 8, WIDE), F32),
        pltpu.VMEM((NZ, 8, WIDE), F32),
        pltpu.VMEM((NX, 2, 8, E), F32),
        pltpu.VMEM((NX, 2, 8, E), F32),
        pltpu.VMEM((2, HALF, E), F32),
        pltpu.VMEM((2, 2, HALF, E), F32),
        pltpu.VMEM((2, HALF, E), F32),
        pltpu.VMEM((2, R, WIDE), F32),
        pltpu.VMEM((NCOL, R, WIDE), F32),
        pltpu.VMEM((R, HALF, E), BF16),
        pltpu.SemaphoreType.DMA((6,)),
        pltpu.SemaphoreType.DMA((N_SEM,)),
        pltpu.SemaphoreType.DMA((N_SEM,)),
    ]
    return pl.pallas_call(
        kernel,
        out_shape=jax.ShapeDtypeStruct((R, C, D), BF16),
        in_specs=[hbm, hbm, hbm, vmem, vmem, vmem, hbm],
        out_specs=hbm,
        scratch_shapes=scratch,
        compiler_params=pltpu.CompilerParams(
            collective_id=0, has_side_effects=True, vmem_limit_bytes=60 * 1024 * 1024),
    )(xin, gate_in, w_proj, rate, skip.reshape(1, E), norm_gain.reshape(1, E), w_out)


def solution(mesh):
    in_specs = (P("rows", "cols", None), P("rows", "cols", None), P(), P(), P(), P(), P())
    return jax.shard_map(local, mesh=mesh, in_specs=in_specs, out_specs=P("rows", "cols", None), check_vma=False)
```

time: 1370 us -> 58 us (0.04)
  the two profiles are of different devices: /device:TPU:136 before, /device:TPU:1 now
where the time goes in v1:
time: 58 us; the launch traced here: 57.8 us
  Pallas kernels  56 us (97%)
  local copies, waits for them, and re-layouts  1.87 us (3%)
    pallas_call x1, Pallas kernels, local(): pl.pallas_call(kernel, out_shape=jax.ShapeDtypeStruct((R, C, D), BF16), i...  56 us
    unnamed x1, local copies, waits for them, and re-layouts  1.87 us

profile of v1, /device:TPU:1, one launch (start us, length us, event | category | flops | bytes accessed | tf_op | source)
XLA Modules:
  0.0 57.8 jit_solution(13354565209463067743)
XLA Ops:
  0.0 56.0 %shard_map.73 = bf16[8,64,512]{2,1,0:T(8,128)(2,1)} custom-call(bf16[8,64,1024]{2,1,0:T(8,128)(2,1)} %x_hbm.1, bf16[8,64,1024]{2,1,0:T(8,128)(2,1)} %g_hbm.1, bf16[1024,128]{1,0:T(8,128)(2,1)} %wp_hbm.1, f32[4,16]{1,0:T(4,128)} %rate_ref.1, f32[1,1024]{1,0:T(1,128)} %bitcast.2, f32[1,1024]{1,0:T(1,128)} %bitcast.3, bf16[1024,512]{1,0:T(8,128)(2,1)} %wo_hbm.1), custom_call_target="tpu_custom_call" | custom-call | tf_op jit(solution)/shard_map/pallas_call | solution.py:402
  56.0 1.9 %copy.9 = bf16[8,64,512]{2,1,0:T(8,128)(2,1)} copy(bf16[8,64,512]{2,1,0:T(8,128)(2,1)} %shard_map.73) | data formatting | bytes 1048576

commit v2 on v1

--- a/solution.py
+++ b/solution.py
@@ -20,10 +20,11 @@
 NB = 256
 CHUNKS = E // NB
 ZERO_ROW = 112
+RS = 72
 
 NZ, NX, NCORE, NCOL = 4, 4, 2, 8
 
-S_CORE, S_X, S_COLS, S_Z, S_BACK, S_LAST, N_SEM = 0, 1, 4, 11, 14, 17, 18
+S_CORE, S_X, S_COLS, S_Z, S_BACK, S_LAST, N_SEM = 0, 2, 8, 15, 18, 24, 26
 
 
 def split(v):
@@ -38,7 +39,7 @@
 
 def kernel(x_hbm, g_hbm, wp_hbm, rate_ref, skip_ref, gain_ref, wo_hbm, o_hbm,
            xb, gb, wp, wo, ob, zsel, c1f, v_hl, d_hl, c1_hl, l_hl, h_hl, fv,
-           x32, base, ro2, ro3, gg, hd0, hb0, ho0, hd1, hb1, ho1,
+           base, ro2, ro3, gg, hd0, hb0, ho0, hd1, hb1, ho1,
            s0, ee, tt, xe, px, gx, tz, ze, sc, rc, fxp, cc, pc, he, hr, nb,
            lsem, ssem, rsem):
     rows = lax.axis_index("rows")
@@ -129,39 +130,40 @@
         v_hl[r] = split(v)
     fv[...] = jnp.exp(up[R - 1])
 
-    def column_ends(start, dst):
+    def column_ends(start, i, dst):
         lhs = v_hl[:, pl.ds(start, HALF), :].reshape(R * HALF, 2 * LANES)
         for n in range(CHUNKS):
             cs = slice(n * NB, (n + 1) * NB)
-            xh = [xb[r, pl.ds(start, HALF), cs].astype(F32) for r in range(R)]
-            for i in range(2):
-                w = mxu(lhs, sel(32 + 16 * i, cs))
-                acc = w[:HALF] * xh[0]
-                for r in range(1, R):
-                    acc = acc + w[r * HALF:(r + 1) * HALF] * xh[r]
-                dst[i, :, cs] = acc
-        for i in range(2):
-            dst[i, :, E:] = fv[pl.ds(start, HALF), :]
+            w = mxu(lhs, sel(32 + 16 * i, cs))
+            acc = w[:HALF] * xb[0, pl.ds(start, HALF), cs].astype(F32)
+            for r in range(1, R):
+                acc = acc + w[r * HALF:(r + 1) * HALF] * xb[r, pl.ds(start, HALF), cs].astype(F32)
+            dst[i, :, cs] = acc
+        dst[i, :, E:] = fv[pl.ds(start, HALF), :]
 
     own = pl.multiple_of(core * HALF, HALF)
     other = pl.multiple_of((1 - core) * HALF, HALF)
-    column_ends(other, s0)
+    to_core = [remote(s0.at[i], ee.at[core, i], S_CORE + i, core_peer) for i in range(2)]
+    column_ends(other, 1, s0)
     pl.semaphore_wait(barrier, len(peers))
-    to_core = remote(s0, ee.at[core], S_CORE, core_peer)
-    to_core.start()
-    column_ends(own, ee.at[core])
-
-    to_core.wait_recv()
-    for i in range(2):
+    to_core[1].start()
+    column_ends(other, 0, s0)
+    to_core[0].start()
+    column_ends(own, 1, ee.at[core])
+    column_ends(own, 0, ee.at[core])
+
+    to_x = [[remote(tt.at[x_dst[d], i], xe.at[xi, i], S_X + 3 * i + d, x_peers[d]) for d in range(NX - 1)]
+            for i in range(2)]
+    for i in (1, 0):
+        to_core[i].wait_recv()
         first, second = ee.at[i, i], ee.at[1 - i, i]
         t = second[:, :E] + spread(second[:, E:], 32 + 16 * i) * first[:, :E]
         f = second[:, E:] * first[:, E:]
         for q in range(NX):
             tt[q, i, :, :E] = t[q * 8:(q + 1) * 8]
             tt[q, i, :, E:] = f[q * 8:(q + 1) * 8]
-    to_x = [remote(tt.at[x_dst[d]], xe.at[xi], S_X + d, x_peers[d]) for d in range(NX - 1)]
-    for copy in to_x:
-        copy.start()
+        for copy in to_x[i]:
+            copy.start()
     xe[xi] = tt[xi]
 
     bt = lax.broadcasted_iota(jnp.int32, (256, 256), 0)
@@ -203,9 +205,6 @@
         xs = [xb[r, :, cs].astype(F32) for r in range(R)]
         sk = skip_ref[:, cs]
         acc = [sk * xs[r] for r in range(R)]
-        for r in range(R):
-            for t in range(2):
-                x32[2 * n + t, r * C:(r + 1) * C, :] = xs[r][:, t * LANES:(t + 1) * LANES]
         for i in range(2):
             off = 32 + 16 * i
             dd = mxu(d_hl[...], sel(off, cs))
@@ -219,63 +218,95 @@
                 acc[r] = acc[r] + oo[ps] * state
         for r in range(R):
             for t in range(2):
-                base[2 * n + t, r * C:(r + 1) * C, :] = acc[r][:, t * LANES:(t + 1) * LANES]
+                base[2 * n + t, r * RS:r * RS + C, :] = acc[r][:, t * LANES:(t + 1) * LANES]
         return 0
 
     lax.fori_loop(0, CHUNKS, column_scans, 0)
 
-    def spread_all(n, _):
-        cs = chunk(n)
-        dv = d_hl[...]
-        cv = c1_hl[...]
-        vv = v_hl[...].reshape(PX, 2 * LANES)
-        for lhs, off, dst in ((dv, 0, hd0), (cv, 0, hb0), (cv, 64, ho0), (dv, 16, hd1), (cv, 16, hb1),
-                              (cv, 80, ho1), (vv, 96, ro2), (vv, 112, ro3)):
-            w = mxu(lhs, sel(off, cs))
-            for t in range(2):
-                dst[2 * n + t] = w[:, t * LANES:(t + 1) * LANES]
-        return 0
-
-    lax.fori_loop(0, CHUNKS, spread_all, 0)
-    load_g.wait()
-
-    def gates(n, _):
-        cs = chunk(n)
-        gain = gain_ref[:, cs]
-        for r in range(R):
-            g = gb[r, :, cs].astype(F32)
-            w = gain * (g / (1.0 + jnp.exp(-g)))
-            for t in range(2):
-                gg[2 * n + t, r * C:(r + 1) * C, :] = w[:, t * LANES:(t + 1) * LANES]
-        return 0
-
-    lax.fori_loop(0, CHUNKS, gates, 0)
-
-    for i in range(2):
-        fxp[i] = spread(ee[i, i, :, E:], 32 + 16 * i)
-
-    for copy in to_x:
-        copy.wait_recv()
-    fc = xe[0, 0, :, E:]
-    for q in range(1, NX):
-        fc = fc * xe[q, 0, :, E:]
-    for i in range(2):
+    to_z = [remote(tz.at[(zi + d) // NZ], ze.at[zi], S_Z + d - 1, z_peers[d - 1]) for d in range(1, NZ)]
+    for i in (1, 0):
+        for copy in to_x[i]:
+            copy.wait_recv()
+        fc = xe[0, i, :, E:]
+        for q in range(1, NX):
+            fc = fc * xe[q, i, :, E:]
         fs = spread(xe[:, i, :, E:].reshape(NX * 8, LANES), 32 + 16 * i)
         acc = jnp.zeros((8, E), F32)
         g = jnp.ones((8, E), F32)
         for q in (range(NX) if i == 0 else range(NX - 1, -1, -1)):
             f = fs[q * 8:(q + 1) * 8]
-            px[q, i] = acc
-            gx[q, i] = g
+            px[i, q] = acc
+            gx[i, q] = g
             acc = xe[q, i, :, :E] + f * acc
             g = g * f
         tz[i, :, :E] = acc
         tz[i, :, E:] = fc
-    to_z = [remote(tz.at[(zi + d) // NZ], ze.at[zi], S_Z + d - 1, z_peers[d - 1]) for d in range(1, NZ)]
-    for copy in to_z:
-        copy.start()
+        for d in range(1, NZ):
+            @pl.when((zi + d) // NZ == i)
+            def _():
+                to_z[d - 1].start()
     ze[zi] = tz[0]
 
+    for i in range(2):
+        fxp[i] = spread(ee[i, i, :, E:], 32 + 16 * i)
+
+    def back_copies(i, order):
+        return [remote(sc.at[i, x_dst[d]], rc.at[i, xi], S_BACK + 3 * order + d, x_peers[d]) for d in range(NX - 1)]
+
+    def over_groups(i, order):
+        for d in range(1, NZ):
+            @pl.when(1 - (zi + NZ - d) // NZ == i)
+            def _():
+                to_z[d - 1].wait_recv()
+        before = zi + i * (NZ - 1 - 2 * zi)
+        slots = []
+        for m in range(NZ - 1):
+            valid = (before + NZ - 1 - m) // NZ
+            slots.append(valid * (m + i * (NZ - 1 - 2 * m)) + (1 - valid) * zi)
+        at = pl.multiple_of(ZERO_ROW - 32 - 16 * i, 16)
+        part = zsel[pl.ds(at, LANES), :]
+        lhs = jnp.concatenate([ze[j, :, E:] for j in slots], axis=0)
+        fs = mxu(split(lhs), jnp.concatenate([part, part], axis=0))
+        acc = jnp.zeros((8, E), F32)
+        for m, j in enumerate(slots):
+            acc = jnp.where(m < before, ze[j, :, :E] + fs[m * 8:(m + 1) * 8] * acc, acc)
+        for q in range(NX):
+            sc[i, q] = px[i, q] + gx[i, q] * acc
+        for copy in back_copies(i, order):
+            copy.start()
+        rc[i, xi] = sc[i, xi]
+
+    def to_last(i, order):
+        return remote(cc.at[1 - core, i], pc.at[i], S_LAST + order, core_peer)
+
+    def over_chip(i, order):
+        for copy in back_copies(i, order):
+            copy.wait_recv()
+        carry = rc[i].reshape(HALF, E)
+        cc[i, i] = carry
+        cc[1 - i, i] = ee[i, i, :, :E] + fxp[i] * carry
+        to_last(i, order).start()
+
+    near = zi // (NZ // 2)
+    far = 1 - near
+    over_groups(near, 0)
+
+    def row_spread(n, _):
+        cs = chunk(n)
+        dv = d_hl[...]
+        cv = c1_hl[...]
+        xs = xb[:, :, cs].astype(F32)
+        for lhs, off, drive, dst in ((dv, 0, 0, hd0), (cv, 0, 1, hb0), (cv, 64, 0, ho0),
+                                     (dv, 16, 0, hd1), (cv, 16, 1, hb1), (cv, 80, 0, ho1)):
+            w = mxu(lhs, sel(off, cs)).reshape(R, C, NB)
+            if drive:
+                w = w * xs
+            for r in range(R):
+                for t in range(2):
+                    dst[2 * n + t, r * RS:r * RS + C, :] = w[r, :, t * LANES:(t + 1) * LANES]
+        return 0
+
+    lax.fori_loop(0, CHUNKS, row_spread, 0)
     for copy in to_cols:
         copy.wait_recv()
     fh = hr[:, :, E:].reshape(NCOL * R, LANES)
@@ -291,73 +322,72 @@
     def row_step(c, states):
         out = []
         for at, hd, hb, ho, first in ((c, hd0, hb0, ho0, 0), (C - 1 - c, hd1, hb1, ho1, TILES)):
-            ps = pl.ds(at, R, stride=C)
+            ps = pl.ds(at, R, stride=RS)
             for t in range(TILES):
-                s = hd[t, ps, :] * states[first + t] + hb[t, ps, :] * x32[t, ps, :]
+                s = hd[t, ps, :] * states[first + t] + hb[t, ps, :]
                 base[t, ps, :] = base[t, ps, :] + ho[t, ps, :] * s
                 out.append(s)
         return tuple(out)
 
-    start = [in0[:, t * LANES:(t + 1) * LANES] for t in range(TILES)]
-    start += [in1[:, t * LANES:(t + 1) * LANES] for t in range(TILES)]
-    lax.fori_loop(0, C, row_step, tuple(start))
+    begin = [in0[:, t * LANES:(t + 1) * LANES] for t in range(TILES)]
+    begin += [in1[:, t * LANES:(t + 1) * LANES] for t in range(TILES)]
+    lax.fori_loop(0, C, row_step, tuple(begin))
+
+    over_chip(near, 0)
+    over_groups(far, 1)
+
+    load_g.wait()
     load_wo.wait()
 
-    for copy in to_z:
-        copy.wait_recv()
-    fz = ze[:, :, E:].reshape(NZ * 8, LANES)
-    for i in range(2):
-        fs = spread(fz, 32 + 16 * i)
-        acc = jnp.zeros((8, E), F32)
-        for j in (range(NZ) if i == 0 else range(NZ - 1, -1, -1)):
-            use = (j < zi) if i == 0 else (j > zi)
-            acc = jnp.where(use, ze[j, :, :E] + fs[j * 8:(j + 1) * 8] * acc, acc)
-        for q in range(NX):
-            sc[q, i] = px[q, i] + gx[q, i] * acc
-    to_back = [remote(sc.at[x_dst[d]], rc.at[xi], S_BACK + d, x_peers[d]) for d in range(NX - 1)]
-    for copy in to_back:
-        copy.start()
-    rc[xi] = sc[xi]
-    for copy in to_back:
-        copy.wait_recv()
-
-    for i in range(2):
-        for q in range(NX):
-            qs = slice(q * 8, (q + 1) * 8)
-            carry = rc[q, i]
-            cc[i, i, qs, :] = carry
-            cc[1 - i, i, qs, :] = ee[i, i, qs, :E] + fxp[i, qs, :] * carry
-    to_last = remote(cc.at[1 - core], pc, S_LAST, core_peer)
-    to_last.start()
+    def tail_spread(n, _):
+        cs = chunk(n)
+        gain = gain_ref[:, cs]
+        vv = v_hl[...].reshape(PX, 2 * LANES)
+        for off, dst in ((96, ro2), (112, ro3)):
+            w = mxu(vv, sel(off, cs))
+            for r in range(R):
+                for t in range(2):
+                    dst[2 * n + t, r * RS:r * RS + C, :] = w[r * C:(r + 1) * C, t * LANES:(t + 1) * LANES]
+        for r in range(R):
+            g = gb[r, :, cs].astype(F32)
+            w = gain * (g / (1.0 + jnp.exp(-g)))
+            for t in range(2):
+                gg[2 * n + t, r * RS:r * RS + C, :] = w[:, t * LANES:(t + 1) * LANES]
+        return 0
+
+    lax.fori_loop(0, CHUNKS, tail_spread, 0)
+    over_chip(far, 1)
 
     def finish(start, carry, number):
-        def line(r, _):
-            ps = pl.ds(pl.multiple_of(r * C + start, HALF), HALF)
-            tot = []
-            sq = jnp.zeros((HALF, LANES), F32)
-            for t in range(TILES):
-                ls = slice(t * LANES, (t + 1) * LANES)
-                v = base[t, ps, :] + ro2[t, ps, :] * carry[0, :, ls] + ro3[t, ps, :] * carry[1, :, ls]
-                sq = sq + v * v
-                tot.append(v)
-            scale = lax.rsqrt(jnp.sum(sq, axis=-1, keepdims=True) * (1.0 / E) + 1e-05)
-            for t in range(TILES):
-                ls = slice(t * LANES, (t + 1) * LANES)
-                nb[r, :, ls] = (tot[t] * scale * gg[t, ps, :]).astype(BF16)
-            return 0
-
-        lax.fori_loop(0, R, line, 0)
-        res = mxu(nb[...].reshape(R * HALF, E), wo[...])
-        ob[:, pl.ds(start, HALF), :] = res.astype(BF16).reshape(R, HALF, D)
+        for part in range(2):
+            for r in range(part * R // 2, (part + 1) * R // 2):
+                ps = pl.ds(pl.multiple_of(r * RS + start, 8), HALF)
+                tot = []
+                sq = jnp.zeros((HALF, LANES), F32)
+                for t in range(TILES):
+                    ls = slice(t * LANES, (t + 1) * LANES)
+                    v = base[t, ps, :] + ro2[t, ps, :] * carry[0, :, ls] + ro3[t, ps, :] * carry[1, :, ls]
+                    sq = sq + v * v
+                    tot.append(v)
+                scale = lax.rsqrt(jnp.sum(sq, axis=-1, keepdims=True) * (1.0 / E) + 1e-05)
+                for t in range(TILES):
+                    ls = slice(t * LANES, (t + 1) * LANES)
+                    nb[r, :, ls] = (tot[t] * scale * gg[t, ps, :]).astype(BF16)
+            rs = slice(part * R // 2, (part + 1) * R // 2)
+            res = mxu(nb[rs].reshape(R // 2 * HALF, E), wo[...])
+            ob[rs, pl.ds(start, HALF), :] = res.astype(BF16).reshape(R // 2, HALF, D)
         copy = pltpu.make_async_copy(ob.at[:, pl.ds(start, HALF), :], o_hbm.at[:, pl.ds(start, HALF), :], lsem.at[number])
         copy.start()
         return copy
 
     out_own = finish(own, cc.at[core], 4)
-    to_last.wait_recv()
+    for order, i in ((0, near), (1, far)):
+        to_last(i, order).wait_recv()
     out_other = finish(other, pc, 5)
-    for copy in [to_core, to_last] + to_x + to_cols + to_z + to_back:
+    for copy in to_core + to_x[0] + to_x[1] + to_cols + to_z + back_copies(near, 0) + back_copies(far, 1):
         copy.wait_send()
+    to_last(near, 0).wait_send()
+    to_last(far, 1).wait_send()
     out_own.wait()
     out_other.wait()
 
@@ -365,7 +395,7 @@
 def local(xin, gate_in, w_proj, rate, skip, norm_gain, w_out):
     vmem = pl.BlockSpec(memory_space=pltpu.VMEM)
     hbm = pl.BlockSpec(memory_space=pl.ANY)
-    big = pltpu.VMEM((TILES, PX, LANES), F32)
+    big = pltpu.VMEM((TILES, R * RS, LANES), F32)
     compact = pltpu.VMEM((PX, 2 * LANES), BF16)
     scratch = [
         pltpu.VMEM((R, C, E), BF16),
@@ -378,17 +408,17 @@
         pltpu.VMEM((R, C, 2 * LANES), BF16),
         compact, compact, compact, compact,
         pltpu.VMEM((C, LANES), F32),
-        big, big, big, big, big, big, big, big, big, big, big,
+        big, big, big, big, big, big, big, big, big, big,
         pltpu.VMEM((2, HALF, WIDE), F32),
         pltpu.VMEM((2, 2, HALF, WIDE), F32),
         pltpu.VMEM((NX, 2, 8, WIDE), F32),
         pltpu.VMEM((NX, 2, 8, WIDE), F32),
-        pltpu.VMEM((NX, 2, 8, E), F32),
-        pltpu.VMEM((NX, 2, 8, E), F32),
+        pltpu.VMEM((2, NX, 8, E), F32),
+        pltpu.VMEM((2, NX, 8, E), F32),
         pltpu.VMEM((2, 8, WIDE), F32),
         pltpu.VMEM((NZ, 8, WIDE), F32),
-        pltpu.VMEM((NX, 2, 8, E), F32),
-        pltpu.VMEM((NX, 2, 8, E), F32),
+        pltpu.VMEM((2, NX, 8, E), F32),
+        pltpu.VMEM((2, NX, 8, E), F32),
         pltpu.VMEM((2, HALF, E), F32),
         pltpu.VMEM((2, 2, HALF, E), F32),
         pltpu.VMEM((2, HALF, E), F32),

time: 58 us -> 35.8 us (0.62)
  Pallas kernels: 56 us -> 33.4 us
    pallas_call x1, Pallas kernels: 56 us -> 33.4 us  [local(): pl.pallas_call(kernel, out_shape=jax.ShapeDtypeStruct((R, C, D), BF16), i...]
where the time goes in v2:
time: 35.8 us; the launch traced here: 35.3 us
  Pallas kernels  33.4 us (93%)
  local copies, waits for them, and re-layouts  1.87 us (5%)
    pallas_call x1, Pallas kernels, local(): pl.pallas_call(kernel, out_shape=jax.ShapeDtypeStruct((R, C, D), BF16), i...  33.4 us
    unnamed x1, local copies, waits for them, and re-layouts  1.87 us

profile of v2, /device:TPU:1, one launch (start us, length us, event | category | flops | bytes accessed | tf_op | source)
XLA Modules:
  0.0 35.3 jit_solution(14395376910002380463)
XLA Ops:
  0.0 33.4 %shard_map.73 = bf16[8,64,512]{2,1,0:T(8,128)(2,1)} custom-call(bf16[8,64,1024]{2,1,0:T(8,128)(2,1)} %x_hbm.1, bf16[8,64,1024]{2,1,0:T(8,128)(2,1)} %g_hbm.1, bf16[1024,128]{1,0:T(8,128)(2,1)} %wp_hbm.1, f32[4,16]{1,0:T(4,128)} %rate_ref.1, f32[1,1024]{1,0:T(1,128)} %bitcast.2, f32[1,1024]{1,0:T(1,128)} %bitcast.3, bf16[1024,512]{1,0:T(8,128)(2,1)} %wo_hbm.1), custom_call_target="tpu_custom_call" | custom-call | tf_op jit(solution)/shard_map/pallas_call | solution.py:432
  33.4 1.9 %copy.9 = bf16[8,64,512]{2,1,0:T(8,128)(2,1)} copy(bf16[8,64,512]{2,1,0:T(8,128)(2,1)} %shard_map.73) | data formatting | bytes 1048576

commit v3 on v2

--- a/solution.py
+++ b/solution.py
@@ -37,8 +37,8 @@
     return jnp.dot(a, b, preferred_element_type=F32)
 
 
-def kernel(x_hbm, g_hbm, wp_hbm, rate_ref, skip_ref, gain_ref, wo_hbm, o_hbm,
-           xb, gb, wp, wo, ob, zsel, c1f, v_hl, d_hl, c1_hl, l_hl, h_hl, fv,
+def kernel(x_hbm, g_hbm, wp_hbm, rate_ref, skip_ref, gain_ref, wo_hbm, ob,
+           xb, gb, wp, wo, zsel, c1f, v_hl, d_hl, c1_hl, l_hl, h_hl, fv,
            base, ro2, ro3, gg, hd0, hb0, ho0, hd1, hb1, ho1,
            s0, ee, tt, xe, px, gx, tz, ze, sc, rc, fxp, cc, pc, he, hr, nb,
            lsem, ssem, rsem):
@@ -144,27 +144,9 @@
     own = pl.multiple_of(core * HALF, HALF)
     other = pl.multiple_of((1 - core) * HALF, HALF)
     to_core = [remote(s0.at[i], ee.at[core, i], S_CORE + i, core_peer) for i in range(2)]
-    column_ends(other, 1, s0)
-    pl.semaphore_wait(barrier, len(peers))
-    to_core[1].start()
-    column_ends(other, 0, s0)
-    to_core[0].start()
-    column_ends(own, 1, ee.at[core])
-    column_ends(own, 0, ee.at[core])
-
-    to_x = [[remote(tt.at[x_dst[d], i], xe.at[xi, i], S_X + 3 * i + d, x_peers[d]) for d in range(NX - 1)]
-            for i in range(2)]
     for i in (1, 0):
-        to_core[i].wait_recv()
-        first, second = ee.at[i, i], ee.at[1 - i, i]
-        t = second[:, :E] + spread(second[:, E:], 32 + 16 * i) * first[:, :E]
-        f = second[:, E:] * first[:, E:]
-        for q in range(NX):
-            tt[q, i, :, :E] = t[q * 8:(q + 1) * 8]
-            tt[q, i, :, E:] = f[q * 8:(q + 1) * 8]
-        for copy in to_x[i]:
-            copy.start()
-    xe[xi] = tt[xi]
+        column_ends(other, i, s0)
+        column_ends(own, i, ee.at[core])
 
     bt = lax.broadcasted_iota(jnp.int32, (256, 256), 0)
     bs = lax.broadcasted_iota(jnp.int32, (256, 256), 1)
@@ -194,6 +176,39 @@
     lax.fori_loop(0, CHUNKS, row_ends, 0)
     for i in range(2):
         he[i, :, E:] = ft
+    pl.semaphore_wait(barrier, len(peers))
+    for i in (1, 0):
+        to_core[i].start()
+
+    load_g.wait()
+    load_wo.wait()
+
+    def gates(n, _):
+        cs = chunk(n)
+        gain = gain_ref[:, cs]
+        for r in range(R):
+            g = gb[r, :, cs].astype(F32)
+            w = gain * (g / (1.0 + jnp.exp(-g)))
+            for t in range(2):
+                gg[2 * n + t, r * RS:r * RS + C, :] = w[:, t * LANES:(t + 1) * LANES]
+        return 0
+
+    lax.fori_loop(0, CHUNKS, gates, 0)
+
+    to_x = [[remote(tt.at[x_dst[d], i], xe.at[xi, i], S_X + 3 * i + d, x_peers[d]) for d in range(NX - 1)]
+            for i in range(2)]
+    for i in (1, 0):
+        to_core[i].wait_recv()
+        first, second = ee.at[i, i], ee.at[1 - i, i]
+        t = second[:, :E] + spread(second[:, E:], 32 + 16 * i) * first[:, :E]
+        f = second[:, E:] * first[:, E:]
+        for q in range(NX):
+            tt[q, i, :, :E] = t[q * 8:(q + 1) * 8]
+            tt[q, i, :, E:] = f[q * 8:(q + 1) * 8]
+        for copy in to_x[i]:
+            copy.start()
+    xe[xi] = tt[xi]
+
     to_cols = [remote(he.at[(col + d) // NCOL], hr.at[col], S_COLS + d - 1, c_peers[d - 1])
                for d in range(1, NCOL)]
     for copy in to_cols:
@@ -222,6 +237,18 @@
         return 0
 
     lax.fori_loop(0, CHUNKS, column_scans, 0)
+
+    def reach_spread(n, _):
+        cs = chunk(n)
+        vv = v_hl[...].reshape(PX, 2 * LANES)
+        for off, dst in ((96, ro2), (112, ro3)):
+            w = mxu(vv, sel(off, cs))
+            for r in range(R):
+                for t in range(2):
+                    dst[2 * n + t, r * RS:r * RS + C, :] = w[r * C:(r + 1) * C, t * LANES:(t + 1) * LANES]
+        return 0
+
+    lax.fori_loop(0, CHUNKS, reach_spread, 0)
 
     to_z = [remote(tz.at[(zi + d) // NZ], ze.at[zi], S_Z + d - 1, z_peers[d - 1]) for d in range(1, NZ)]
     for i in (1, 0):
@@ -289,7 +316,6 @@
 
     near = zi // (NZ // 2)
     far = 1 - near
-    over_groups(near, 0)
 
     def row_spread(n, _):
         cs = chunk(n)
@@ -331,34 +357,14 @@
 
     begin = [in0[:, t * LANES:(t + 1) * LANES] for t in range(TILES)]
     begin += [in1[:, t * LANES:(t + 1) * LANES] for t in range(TILES)]
-    lax.fori_loop(0, C, row_step, tuple(begin))
-
+    states = lax.fori_loop(0, C // 2, row_step, tuple(begin))
+    over_groups(near, 0)
+    over_groups(far, 1)
+    lax.fori_loop(C // 2, C, row_step, states)
     over_chip(near, 0)
-    over_groups(far, 1)
-
-    load_g.wait()
-    load_wo.wait()
-
-    def tail_spread(n, _):
-        cs = chunk(n)
-        gain = gain_ref[:, cs]
-        vv = v_hl[...].reshape(PX, 2 * LANES)
-        for off, dst in ((96, ro2), (112, ro3)):
-            w = mxu(vv, sel(off, cs))
-            for r in range(R):
-                for t in range(2):
-                    dst[2 * n + t, r * RS:r * RS + C, :] = w[r * C:(r + 1) * C, t * LANES:(t + 1) * LANES]
-        for r in range(R):
-            g = gb[r, :, cs].astype(F32)
-            w = gain * (g / (1.0 + jnp.exp(-g)))
-            for t in range(2):
-                gg[2 * n + t, r * RS:r * RS + C, :] = w[:, t * LANES:(t + 1) * LANES]
-        return 0
-
-    lax.fori_loop(0, CHUNKS, tail_spread, 0)
     over_chip(far, 1)
 
-    def finish(start, carry, number):
+    def finish(start, carry):
         for part in range(2):
             for r in range(part * R // 2, (part + 1) * R // 2):
                 ps = pl.ds(pl.multiple_of(r * RS + start, 8), HALF)
@@ -376,20 +382,15 @@
             rs = slice(part * R // 2, (part + 1) * R // 2)
             res = mxu(nb[rs].reshape(R // 2 * HALF, E), wo[...])
             ob[rs, pl.ds(start, HALF), :] = res.astype(BF16).reshape(R // 2, HALF, D)
-        copy = pltpu.make_async_copy(ob.at[:, pl.ds(start, HALF), :], o_hbm.at[:, pl.ds(start, HALF), :], lsem.at[number])
-        copy.start()
-        return copy
-
-    out_own = finish(own, cc.at[core], 4)
+
+    finish(own, cc.at[core])
     for order, i in ((0, near), (1, far)):
         to_last(i, order).wait_recv()
-    out_other = finish(other, pc, 5)
+    finish(other, pc)
     for copy in to_core + to_x[0] + to_x[1] + to_cols + to_z + back_copies(near, 0) + back_copies(far, 1):
         copy.wait_send()
     to_last(near, 0).wait_send()
     to_last(far, 1).wait_send()
-    out_own.wait()
-    out_other.wait()
 
 
 def local(xin, gate_in, w_proj, rate, skip, norm_gain, w_out):
@@ -402,7 +403,6 @@
         pltpu.VMEM((R, C, E), BF16),
         pltpu.VMEM((E, LANES), BF16),
         pltpu.VMEM((E, D), BF16),
-        pltpu.VMEM((R, C, D), BF16),
         pltpu.VMEM((ZERO_ROW + LANES, E), BF16),
         pltpu.VMEM((PX, LANES), F32),
         pltpu.VMEM((R, C, 2 * LANES), BF16),
@@ -431,9 +431,9 @@
     ]
     return pl.pallas_call(
         kernel,
-        out_shape=jax.ShapeDtypeStruct((R, C, D), BF16),
+        out_shape=pltpu.VMEM((R, C, D), BF16),
         in_specs=[hbm, hbm, hbm, vmem, vmem, vmem, hbm],
-        out_specs=hbm,
+        out_specs=vmem,
         scratch_shapes=scratch,
         compiler_params=pltpu.CompilerParams(
             collective_id=0, has_side_effects=True, vmem_limit_bytes=60 * 1024 * 1024),

time: 35.8 us -> 31.8 us (0.89); the launches traced: 35.3 us -> 31.7 us
  Pallas kernels: 33.4 us -> 30.9 us
  local copies, waits for them, and re-layouts: 1.87 us -> 0.8 us
    pallas_call x1, Pallas kernels: 33.4 us -> 30.9 us  [local(): pl.pallas_call(kernel, out_shape=pltpu.VMEM((R, C, D), BF16), in_specs=[h...]
    unnamed x1, local copies, waits for them, and re-layouts: 1.87 us -> 0.8 us
where the time goes in v3:
time: 31.8 us; the launch traced here: 31.7 us
  Pallas kernels  30.9 us (97%)
  local copies, waits for them, and re-layouts  0.8 us (3%)
    pallas_call x1, Pallas kernels, local(): pl.pallas_call(kernel, out_shape=pltpu.VMEM((R, C, D), BF16), in_specs=[h...  30.9 us
    unnamed x1, local copies, waits for them, and re-layouts  0.8 us

profile of v3, /device:TPU:1, one launch (start us, length us, event | category | flops | bytes accessed | tf_op | source)
XLA Modules:
  0.0 31.7 jit_solution(2169464614787042292)
XLA Ops:
  0.0 30.9 %shard_map.73 = bf16[8,64,512]{2,1,0:T(8,128)(2,1)S(1)} custom-call(bf16[8,64,1024]{2,1,0:T(8,128)(2,1)} %x_hbm.1, bf16[8,64,1024]{2,1,0:T(8,128)(2,1)} %g_hbm.1, bf16[1024,128]{1,0:T(8,128)(2,1)} %wp_hbm.1, f32[4,16]{1,0:T(4,128)} %rate_ref.1, f32[1,1024]{1,0:T(1,128)} %bitcast.2, f32[1,1024]{1,0:T(1,128)} %bitcast.3, bf16[1024,512]{1,0:T(8,128)(2,1)} %wo_hbm.1), custom_call_target="tpu_custom_call" | custom-call | tf_op jit(solution)/shard_map/pallas_call | solution.py:432
  30.9 0.8 %copy.9 = bf16[8,64,512]{2,1,0:T(8,128)(2,1)} copy(bf16[8,64,512]{2,1,0:T(8,128)(2,1)S(1)} %shard_map.73) | data formatting | bytes 1048576

commit v4 on v3

--- a/solution.py
+++ b/solution.py
@@ -23,6 +23,7 @@
 RS = 72
 
 NZ, NX, NCORE, NCOL = 4, 4, 2, 8
+FAR_FIRST = (1, 0, 2)
 
 S_CORE, S_X, S_COLS, S_Z, S_BACK, S_LAST, N_SEM = 0, 2, 8, 15, 18, 24, 26
 
@@ -37,8 +38,8 @@
     return jnp.dot(a, b, preferred_element_type=F32)
 
 
-def kernel(x_hbm, g_hbm, wp_hbm, rate_ref, skip_ref, gain_ref, wo_hbm, ob,
-           xb, gb, wp, wo, zsel, c1f, v_hl, d_hl, c1_hl, l_hl, h_hl, fv,
+def kernel(x_hbm, g_hbm, wp_hbm, rate_hbm, skip_hbm, gain_hbm, wo_hbm, ob,
+           xb, gb, wp, wo, rate_ref, skip_ref, gain_ref, zsel, c1f, v_hl, d_hl, c1_hl, l_hl, h_hl, fv,
            base, ro2, ro3, gg, hd0, hb0, ho0, hd1, hb1, ho1,
            s0, ee, tt, xe, px, gx, tz, ze, sc, rc, fxp, cc, pc, he, hr, nb,
            lsem, ssem, rsem):
@@ -63,8 +64,14 @@
     load_x = pltpu.make_async_copy(x_hbm, xb, lsem.at[1])
     load_g = pltpu.make_async_copy(g_hbm, gb, lsem.at[2])
     load_wo = pltpu.make_async_copy(wo_hbm, wo, lsem.at[3])
+    load_rate = pltpu.make_async_copy(rate_hbm, rate_ref, lsem.at[4])
+    load_skip = pltpu.make_async_copy(skip_hbm, skip_ref, lsem.at[5])
+    load_gain = pltpu.make_async_copy(gain_hbm, gain_ref, lsem.at[6])
     load_wp.start()
     load_x.start()
+    load_rate.start()
+    load_skip.start()
+    load_gain.start()
     load_g.start()
     load_wo.start()
 
@@ -87,6 +94,20 @@
 
     def spread(v, off):
         return mxu(split(v), sel(off, slice(0, E)))
+
+    low = lax.broadcasted_iota(jnp.int32, (8, LANES), 1) < 64
+
+    def spread_few(v, off):
+        out = []
+        for m in range(v.shape[0] // 8):
+            row = v[m * 8:(m + 1) * 8]
+            tiles = []
+            for t in range(TILES):
+                a = jnp.broadcast_to(row[:, off + 2 * t:off + 2 * t + 1], (8, LANES))
+                b = jnp.broadcast_to(row[:, off + 2 * t + 1:off + 2 * t + 2], (8, LANES))
+                tiles.append(jnp.where(low, a, b))
+            out.append(jnp.concatenate(tiles, axis=1))
+        return jnp.concatenate(out, axis=0)
 
     src_lane = lax.broadcasted_iota(jnp.int32, (LANES, 2 * LANES), 0)
     lane = lax.broadcasted_iota(jnp.int32, (LANES, 2 * LANES), 1)
@@ -94,10 +115,11 @@
     h = within % 16
     want = 32 * (within // 16) + jnp.where(lane < 128, h, jnp.where(lane < 192, 16 + h // 2, 24 + h // 2))
     pick = (src_lane == want).astype(F32).astype(BF16)
+    load_wp.wait()
+    w2 = mxu(wp[...], pick).astype(BF16)
+    load_rate.wait()
     rate = rate_ref[...]
     rate_lane = jnp.concatenate([rate[k:k + 1, :] for k in range(4)] * 2, axis=1)
-    load_wp.wait()
-    w2 = mxu(wp[...], pick).astype(BF16)
     load_x.wait()
     proj = mxu(xb[...].reshape(PX, E), w2)
     pre = proj[:, :LANES]
@@ -144,9 +166,7 @@
     own = pl.multiple_of(core * HALF, HALF)
     other = pl.multiple_of((1 - core) * HALF, HALF)
     to_core = [remote(s0.at[i], ee.at[core, i], S_CORE + i, core_peer) for i in range(2)]
-    for i in (1, 0):
-        column_ends(other, i, s0)
-        column_ends(own, i, ee.at[core])
+    column_ends(other, 1, s0)
 
     bt = lax.broadcasted_iota(jnp.int32, (256, 256), 0)
     bs = lax.broadcasted_iota(jnp.int32, (256, 256), 1)
@@ -166,6 +186,11 @@
     ft = mxu(whole, l_hl[...])
     ft = jnp.exp(ft[:, :LANES] + ft[:, LANES:])
 
+    first = (NZ - zi) // NZ
+    r_early = CHUNKS * ((NZ - 1 - zi) // (NZ // 2))
+    c_early = CHUNKS // 2 * (first + (NZ - 1 - zi) // (NZ // 2))
+    g_early = CHUNKS * first
+
     def row_ends(n, _):
         cs = chunk(n)
         for i in range(2):
@@ -173,47 +198,12 @@
             he[i, :, cs] = jnp.sum(w * xb[:, :, cs].astype(F32), axis=1)
         return 0
 
-    lax.fori_loop(0, CHUNKS, row_ends, 0)
+    lax.fori_loop(0, r_early, row_ends, 0)
     for i in range(2):
         he[i, :, E:] = ft
-    pl.semaphore_wait(barrier, len(peers))
-    for i in (1, 0):
-        to_core[i].start()
-
-    load_g.wait()
-    load_wo.wait()
-
-    def gates(n, _):
-        cs = chunk(n)
-        gain = gain_ref[:, cs]
-        for r in range(R):
-            g = gb[r, :, cs].astype(F32)
-            w = gain * (g / (1.0 + jnp.exp(-g)))
-            for t in range(2):
-                gg[2 * n + t, r * RS:r * RS + C, :] = w[:, t * LANES:(t + 1) * LANES]
-        return 0
-
-    lax.fori_loop(0, CHUNKS, gates, 0)
-
-    to_x = [[remote(tt.at[x_dst[d], i], xe.at[xi, i], S_X + 3 * i + d, x_peers[d]) for d in range(NX - 1)]
-            for i in range(2)]
-    for i in (1, 0):
-        to_core[i].wait_recv()
-        first, second = ee.at[i, i], ee.at[1 - i, i]
-        t = second[:, :E] + spread(second[:, E:], 32 + 16 * i) * first[:, :E]
-        f = second[:, E:] * first[:, E:]
-        for q in range(NX):
-            tt[q, i, :, :E] = t[q * 8:(q + 1) * 8]
-            tt[q, i, :, E:] = f[q * 8:(q + 1) * 8]
-        for copy in to_x[i]:
-            copy.start()
-    xe[xi] = tt[xi]
-
-    to_cols = [remote(he.at[(col + d) // NCOL], hr.at[col], S_COLS + d - 1, c_peers[d - 1])
-               for d in range(1, NCOL)]
-    for copy in to_cols:
-        copy.start()
-    hr[col] = he[0]
+
+    load_skip.wait()
+    load_gain.wait()
 
     def column_scans(n, _):
         cs = chunk(n)
@@ -236,7 +226,56 @@
                 base[2 * n + t, r * RS:r * RS + C, :] = acc[r][:, t * LANES:(t + 1) * LANES]
         return 0
 
-    lax.fori_loop(0, CHUNKS, column_scans, 0)
+    lax.fori_loop(0, c_early, column_scans, 0)
+    load_g.wait()
+    load_wo.wait()
+
+    def gates(n, _):
+        cs = chunk(n)
+        gain = gain_ref[:, cs]
+        for r in range(R):
+            g = gb[r, :, cs].astype(F32)
+            w = gain * (g / (1.0 + jnp.exp(-g)))
+            for t in range(2):
+                gg[2 * n + t, r * RS:r * RS + C, :] = w[:, t * LANES:(t + 1) * LANES]
+        return 0
+
+    lax.fori_loop(0, g_early, gates, 0)
+
+    pl.semaphore_wait(barrier, len(peers))
+    to_core[1].start()
+    column_ends(other, 0, s0)
+    to_core[0].start()
+    column_ends(own, 1, ee.at[core])
+    column_ends(own, 0, ee.at[core])
+
+
+    to_x = [[remote(tt.at[x_dst[d], i], xe.at[xi, i], S_X + 3 * i + d, x_peers[d]) for d in range(NX - 1)]
+            for i in range(2)]
+
+    def join_cores(i):
+        to_core[i].wait_recv()
+        first, second = ee.at[i, i], ee.at[1 - i, i]
+        t = second[:, :E] + spread_few(second[:, E:], 32 + 16 * i) * first[:, :E]
+        f = second[:, E:] * first[:, E:]
+        for q in range(NX):
+            tt[q, i, :, :E] = t[q * 8:(q + 1) * 8]
+            tt[q, i, :, E:] = f[q * 8:(q + 1) * 8]
+        for d in FAR_FIRST:
+            to_x[i][d].start()
+        xe[xi, i] = tt[xi, i]
+
+    join_cores(1)
+    lax.fori_loop(r_early, CHUNKS, row_ends, 0)
+    to_cols = [remote(he.at[(col + d) // NCOL], hr.at[col], S_COLS + d - 1, c_peers[d - 1])
+               for d in range(1, NCOL)]
+    for copy in to_cols:
+        copy.start()
+    hr[col] = he[0]
+
+    join_cores(0)
+    lax.fori_loop(c_early, CHUNKS, column_scans, 0)
+
 
     def reach_spread(n, _):
         cs = chunk(n)
@@ -248,74 +287,8 @@
                     dst[2 * n + t, r * RS:r * RS + C, :] = w[r * C:(r + 1) * C, t * LANES:(t + 1) * LANES]
         return 0
 
-    lax.fori_loop(0, CHUNKS, reach_spread, 0)
-
-    to_z = [remote(tz.at[(zi + d) // NZ], ze.at[zi], S_Z + d - 1, z_peers[d - 1]) for d in range(1, NZ)]
-    for i in (1, 0):
-        for copy in to_x[i]:
-            copy.wait_recv()
-        fc = xe[0, i, :, E:]
-        for q in range(1, NX):
-            fc = fc * xe[q, i, :, E:]
-        fs = spread(xe[:, i, :, E:].reshape(NX * 8, LANES), 32 + 16 * i)
-        acc = jnp.zeros((8, E), F32)
-        g = jnp.ones((8, E), F32)
-        for q in (range(NX) if i == 0 else range(NX - 1, -1, -1)):
-            f = fs[q * 8:(q + 1) * 8]
-            px[i, q] = acc
-            gx[i, q] = g
-            acc = xe[q, i, :, :E] + f * acc
-            g = g * f
-        tz[i, :, :E] = acc
-        tz[i, :, E:] = fc
-        for d in range(1, NZ):
-            @pl.when((zi + d) // NZ == i)
-            def _():
-                to_z[d - 1].start()
-    ze[zi] = tz[0]
-
-    for i in range(2):
-        fxp[i] = spread(ee[i, i, :, E:], 32 + 16 * i)
-
-    def back_copies(i, order):
-        return [remote(sc.at[i, x_dst[d]], rc.at[i, xi], S_BACK + 3 * order + d, x_peers[d]) for d in range(NX - 1)]
-
-    def over_groups(i, order):
-        for d in range(1, NZ):
-            @pl.when(1 - (zi + NZ - d) // NZ == i)
-            def _():
-                to_z[d - 1].wait_recv()
-        before = zi + i * (NZ - 1 - 2 * zi)
-        slots = []
-        for m in range(NZ - 1):
-            valid = (before + NZ - 1 - m) // NZ
-            slots.append(valid * (m + i * (NZ - 1 - 2 * m)) + (1 - valid) * zi)
-        at = pl.multiple_of(ZERO_ROW - 32 - 16 * i, 16)
-        part = zsel[pl.ds(at, LANES), :]
-        lhs = jnp.concatenate([ze[j, :, E:] for j in slots], axis=0)
-        fs = mxu(split(lhs), jnp.concatenate([part, part], axis=0))
-        acc = jnp.zeros((8, E), F32)
-        for m, j in enumerate(slots):
-            acc = jnp.where(m < before, ze[j, :, :E] + fs[m * 8:(m + 1) * 8] * acc, acc)
-        for q in range(NX):
-            sc[i, q] = px[i, q] + gx[i, q] * acc
-        for copy in back_copies(i, order):
-            copy.start()
-        rc[i, xi] = sc[i, xi]
-
-    def to_last(i, order):
-        return remote(cc.at[1 - core, i], pc.at[i], S_LAST + order, core_peer)
-
-    def over_chip(i, order):
-        for copy in back_copies(i, order):
-            copy.wait_recv()
-        carry = rc[i].reshape(HALF, E)
-        cc[i, i] = carry
-        cc[1 - i, i] = ee[i, i, :, :E] + fxp[i] * carry
-        to_last(i, order).start()
-
-    near = zi // (NZ // 2)
-    far = 1 - near
+    lax.fori_loop(g_early, r_early, gates, 0)
+    lax.fori_loop(0, r_early, reach_spread, 0)
 
     def row_spread(n, _):
         cs = chunk(n)
@@ -332,7 +305,80 @@
                     dst[2 * n + t, r * RS:r * RS + C, :] = w[r, :, t * LANES:(t + 1) * LANES]
         return 0
 
-    lax.fori_loop(0, CHUNKS, row_spread, 0)
+    lax.fori_loop(0, c_early, row_spread, 0)
+
+    to_z = [remote(tz.at[(zi + d) // NZ], ze.at[zi], S_Z + d - 1, z_peers[d - 1]) for d in range(1, NZ)]
+    for i in (1, 0):
+        for copy in to_x[i]:
+            copy.wait_recv()
+        fc = xe[0, i, :, E:]
+        for q in range(1, NX):
+            fc = fc * xe[q, i, :, E:]
+        fs = spread_few(xe[:, i, :, E:].reshape(NX * 8, LANES), 32 + 16 * i)
+        acc = jnp.zeros((8, E), F32)
+        g = jnp.ones((8, E), F32)
+        for q in (range(NX) if i == 0 else range(NX - 1, -1, -1)):
+            f = fs[q * 8:(q + 1) * 8]
+            px[i, q] = acc
+            gx[i, q] = g
+            acc = xe[q, i, :, :E] + f * acc
+            g = g * f
+        tz[i, :, :E] = acc
+        tz[i, :, E:] = pltpu.roll(fc, LANES - 32 - 16 * i, 1)
+        for d in FAR_FIRST:
+            @pl.when((zi + d + 1) // NZ == i)
+            def _():
+                to_z[d].start()
+    ze[zi] = tz[0]
+
+    for i in range(2):
+        fxp[i] = spread(ee[i, i, :, E:], 32 + 16 * i)
+
+    def back_copies(i, order):
+        return [remote(sc.at[i, x_dst[d]], rc.at[i, xi], S_BACK + 3 * order + d, x_peers[d]) for d in range(NX - 1)]
+
+    def over_groups(i, order):
+        for d in range(1, NZ):
+            @pl.when(1 - (zi + NZ - d) // NZ == i)
+            def _():
+                to_z[d - 1].wait_recv()
+        before = zi + i * (NZ - 1 - 2 * zi)
+        slots = []
+        for m in range(NZ - 1):
+            valid = (before + NZ - 1 - m) // NZ
+            slots.append(valid * (m + i * (NZ - 1 - 2 * m)) + (1 - valid) * zi)
+        fs = spread_few(jnp.concatenate([ze[j, :, E:] for j in slots], axis=0), 0)
+        acc = jnp.zeros((8, E), F32)
+        for m, j in enumerate(slots):
+            acc = jnp.where(m < before, ze[j, :, :E] + fs[m * 8:(m + 1) * 8] * acc, acc)
+        for q in range(NX):
+            sc[i, q] = px[i, q] + gx[i, q] * acc
+        copies = back_copies(i, order)
+        for d in FAR_FIRST:
+            copies[d].start()
+        rc[i, xi] = sc[i, xi]
+
+    def to_last(i, order):
+        return remote(cc.at[1 - core, i], pc.at[i], S_LAST + order, core_peer)
+
+    def over_chip(i, order):
+        for copy in back_copies(i, order):
+            copy.wait_recv()
+        carry = rc[i].reshape(HALF, E)
+        cc[i, i] = carry
+        cc[1 - i, i] = ee[i, i, :, :E] + fxp[i] * carry
+        to_last(i, order).start()
+
+    near = zi // (NZ // 2)
+    far = 1 - near
+
+    edge = zi % (NZ - 1) == 0
+
+    @pl.when(edge)
+    def _():
+        over_groups(near, 0)
+
+    lax.fori_loop(c_early, CHUNKS, row_spread, 0)
     for copy in to_cols:
         copy.wait_recv()
     fh = hr[:, :, E:].reshape(NCOL * R, LANES)
@@ -358,10 +404,24 @@
     begin = [in0[:, t * LANES:(t + 1) * LANES] for t in range(TILES)]
     begin += [in1[:, t * LANES:(t + 1) * LANES] for t in range(TILES)]
     states = lax.fori_loop(0, C // 2, row_step, tuple(begin))
-    over_groups(near, 0)
+
+    @pl.when(edge)
+    def _():
+        over_chip(near, 0)
+
+    @pl.when(jnp.logical_not(edge))
+    def _():
+        over_groups(near, 0)
+
     over_groups(far, 1)
     lax.fori_loop(C // 2, C, row_step, states)
-    over_chip(near, 0)
+    lax.fori_loop(r_early, CHUNKS, gates, 0)
+    lax.fori_loop(r_early, CHUNKS, reach_spread, 0)
+
+    @pl.when(jnp.logical_not(edge))
+    def _():
+        over_chip(near, 0)
+
     over_chip(far, 1)
 
     def finish(start, carry):
@@ -403,6 +463,9 @@
         pltpu.VMEM((R, C, E), BF16),
         pltpu.VMEM((E, LANES), BF16),
         pltpu.VMEM((E, D), BF16),
+        pltpu.VMEM((4, HEADS), F32),
+        pltpu.VMEM((1, E), F32),
+        pltpu.VMEM((1, E), F32),
         pltpu.VMEM((ZERO_ROW + LANES, E), BF16),
         pltpu.VMEM((PX, LANES), F32),
         pltpu.VMEM((R, C, 2 * LANES), BF16),
@@ -425,14 +488,14 @@
         pltpu.VMEM((2, R, WIDE), F32),
         pltpu.VMEM((NCOL, R, WIDE), F32),
         pltpu.VMEM((R, HALF, E), BF16),
-        pltpu.SemaphoreType.DMA((6,)),
+        pltpu.SemaphoreType.DMA((7,)),
         pltpu.SemaphoreType.DMA((N_SEM,)),
         pltpu.SemaphoreType.DMA((N_SEM,)),
     ]
     return pl.pallas_call(
         kernel,
         out_shape=pltpu.VMEM((R, C, D), BF16),
-        in_specs=[hbm, hbm, hbm, vmem, vmem, vmem, hbm],
+        in_specs=[hbm] * 7,
         out_specs=vmem,
         scratch_shapes=scratch,
         compiler_params=pltpu.CompilerParams(

time: 31.8 us -> 29.6 us (0.931)
  Pallas kernels: 30.9 us -> 28.7 us
    pallas_call x1, Pallas kernels: 30.9 us -> 28.7 us  [local(): pl.pallas_call(kernel, out_shape=pltpu.VMEM((R, C, D), BF16), in_specs=[h...]
where the time goes in v4:
time: 29.6 us; the launch traced here: 29.5 us
  Pallas kernels  28.7 us (97%)
  local copies, waits for them, and re-layouts  0.8 us (3%)
    pallas_call x1, Pallas kernels, local(): pl.pallas_call(kernel, out_shape=pltpu.VMEM((R, C, D), BF16), in_specs=[h...  28.7 us
    unnamed x1, local copies, waits for them, and re-layouts  0.8 us

profile of v4, /device:TPU:1, one launch (start us, length us, event | category | flops | bytes accessed | tf_op | source)
XLA Modules:
  0.0 29.5 jit_solution(14492591509248794316)
XLA Ops:
  0.0 28.7 %shard_map.73 = bf16[8,64,512]{2,1,0:T(8,128)(2,1)S(1)} custom-call(bf16[8,64,1024]{2,1,0:T(8,128)(2,1)} %x_hbm.1, bf16[8,64,1024]{2,1,0:T(8,128)(2,1)} %g_hbm.1, bf16[1024,128]{1,0:T(8,128)(2,1)} %wp_hbm.1, f32[4,16]{1,0:T(4,128)} %rate_hbm.1, f32[1,1024]{1,0:T(1,128)} %bitcast.2, f32[1,1024]{1,0:T(1,128)} %bitcast.3, bf16[1024,512]{1,0:T(8,128)(2,1)} %wo_hbm.1), custom_call_target="tpu_custom_call" | custom-call | tf_op jit(solution)/shard_map/pallas_call | solution.py:495
  28.7 0.8 %copy.9 = bf16[8,64,512]{2,1,0:T(8,128)(2,1)} copy(bf16[8,64,512]{2,1,0:T(8,128)(2,1)S(1)} %shard_map.73) | data formatting | bytes 1048576

commit v5 on v4

--- a/solution.py
+++ b/solution.py
@@ -15,6 +15,7 @@
 PX = R * C
 HALF = C // 2
 LANES = 128
+PART = 16
 TILES = E // LANES
 WIDE = E + LANES
 NB = 256
@@ -25,7 +26,7 @@
 NZ, NX, NCORE, NCOL = 4, 4, 2, 8
 FAR_FIRST = (1, 0, 2)
 
-S_CORE, S_X, S_COLS, S_Z, S_BACK, S_LAST, N_SEM = 0, 2, 8, 15, 18, 24, 26
+S_CORE, S_X, S_COLS, S_Z, S_BACK, S_LAST, N_SEM = 0, 2, 8, 15, 18, 24, 27
 
 
 def split(v):
@@ -42,7 +43,7 @@
            xb, gb, wp, wo, rate_ref, skip_ref, gain_ref, zsel, c1f, v_hl, d_hl, c1_hl, l_hl, h_hl, fv,
            base, ro2, ro3, gg, hd0, hb0, ho0, hd1, hb1, ho1,
            s0, ee, tt, xe, px, gx, tz, ze, sc, rc, fxp, cc, pc, he, hr, nb,
-           lsem, ssem, rsem):
+           lsem, ssem, rsem, gsem):
     rows = lax.axis_index("rows")
     col = lax.axis_index("cols")
     core = rows % NCORE
@@ -54,11 +55,39 @@
     x_peers = [{"rows": (zi * NX + t) * NCORE + core} for t in x_dst]
     z_peers = [{"rows": (((zi + d) % NZ) * NX + xi) * NCORE + core} for d in range(1, NZ)]
     c_peers = [{"cols": (col + d) % NCOL} for d in range(1, NCOL)]
-    peers = [core_peer] + x_peers + z_peers + c_peers
-
+    def greeter(peer):
+        peer_rows = peer.get("rows", rows)
+        return {"rows": peer_rows - peer_rows % NCORE + 1, "cols": peer.get("cols", col)}
+
+    outside = [greeter(peer) for peer in x_peers + z_peers + c_peers]
     barrier = pltpu.get_barrier_semaphore()
-    for peer in peers:
+
+    @pl.when(core == 1)
+    def _():
+        pl.semaphore_signal(barrier, inc=1, device_id=core_peer, device_id_type=MESH)
+
+    for peer in outside:
         pl.semaphore_signal(barrier, inc=1, device_id=peer, device_id_type=MESH)
+
+    def wait_for_core():
+        @pl.when(core == 0)
+        def _():
+            pl.semaphore_wait(barrier, 1)
+            pl.semaphore_signal(gsem.at[0], inc=1, device_id=core_peer, device_id_type=MESH)
+
+        @pl.when(core == 1)
+        def _():
+            pl.semaphore_wait(gsem.at[0], 1)
+
+    def wait_for_others():
+        @pl.when(core == 1)
+        def _():
+            pl.semaphore_wait(barrier, NCORE * len(outside))
+            pl.semaphore_signal(gsem.at[1], inc=1, device_id=core_peer, device_id_type=MESH)
+
+        @pl.when(core == 0)
+        def _():
+            pl.semaphore_wait(gsem.at[1], 1)
 
     load_wp = pltpu.make_async_copy(wp_hbm, wp, lsem.at[0])
     load_x = pltpu.make_async_copy(x_hbm, xb, lsem.at[1])
@@ -242,7 +271,7 @@
 
     lax.fori_loop(0, g_early, gates, 0)
 
-    pl.semaphore_wait(barrier, len(peers))
+    wait_for_core()
     to_core[1].start()
     column_ends(other, 0, s0)
     to_core[0].start()
@@ -261,6 +290,8 @@
         for q in range(NX):
             tt[q, i, :, :E] = t[q * 8:(q + 1) * 8]
             tt[q, i, :, E:] = f[q * 8:(q + 1) * 8]
+        if i == 1:
+            wait_for_others()
         for d in FAR_FIRST:
             to_x[i][d].start()
         xe[xi, i] = tt[xi, i]
@@ -405,10 +436,6 @@
     begin += [in1[:, t * LANES:(t + 1) * LANES] for t in range(TILES)]
     states = lax.fori_loop(0, C // 2, row_step, tuple(begin))
 
-    @pl.when(edge)
-    def _():
-        over_chip(near, 0)
-
     @pl.when(jnp.logical_not(edge))
     def _():
         over_groups(near, 0)
@@ -417,40 +444,62 @@
     lax.fori_loop(C // 2, C, row_step, states)
     lax.fori_loop(r_early, CHUNKS, gates, 0)
     lax.fori_loop(r_early, CHUNKS, reach_spread, 0)
-
-    @pl.when(jnp.logical_not(edge))
-    def _():
-        over_chip(near, 0)
-
-    over_chip(far, 1)
-
-    def finish(start, carry):
-        for part in range(2):
-            for r in range(part * R // 2, (part + 1) * R // 2):
-                ps = pl.ds(pl.multiple_of(r * RS + start, 8), HALF)
-                tot = []
-                sq = jnp.zeros((HALF, LANES), F32)
-                for t in range(TILES):
-                    ls = slice(t * LANES, (t + 1) * LANES)
-                    v = base[t, ps, :] + ro2[t, ps, :] * carry[0, :, ls] + ro3[t, ps, :] * carry[1, :, ls]
-                    sq = sq + v * v
-                    tot.append(v)
-                scale = lax.rsqrt(jnp.sum(sq, axis=-1, keepdims=True) * (1.0 / E) + 1e-05)
-                for t in range(TILES):
-                    ls = slice(t * LANES, (t + 1) * LANES)
-                    nb[r, :, ls] = (tot[t] * scale * gg[t, ps, :]).astype(BF16)
-            rs = slice(part * R // 2, (part + 1) * R // 2)
-            res = mxu(nb[rs].reshape(R // 2 * HALF, E), wo[...])
-            ob[rs, pl.ds(start, HALF), :] = res.astype(BF16).reshape(R // 2, HALF, D)
-
-    finish(own, cc.at[core])
-    for order, i in ((0, near), (1, far)):
-        to_last(i, order).wait_recv()
-    finish(other, pc)
+    over_chip(near, 0)
+
+    odd = xi % 2
+
+    def arrived(d):
+        remote(sc.at[far, xi], rc.at[far, xi], S_BACK + 3 + d, x_peers[1]).wait_recv()
+
+    def last_part(p):
+        cs = pl.ds(starts[p], PART)
+        return remote(cc.at[1 - core, far, cs], pc.at[far, cs], S_LAST + 1 + p, core_peer)
+
+    def over_chip_part(p):
+        cs = pl.ds(starts[p], PART)
+        carry = rc[far, pl.ds(starts[p] // 8, PART // 8)].reshape(PART, E)
+        cc[far, far, cs, :] = carry
+        cc[1 - far, far, cs, :] = ee[far, far, cs, :E] + fxp[far, cs, :] * carry
+        last_part(p).start()
+
+    group = xi // 2
+    starts = [pl.multiple_of(group * PART, PART), pl.multiple_of((1 - group) * PART, PART)]
+
+    def finish(start, carry, p):
+        cs = pl.ds(starts[p], PART)
+        for r in range(R):
+            ps = pl.ds(pl.multiple_of(r * RS + start + starts[p], 8), PART)
+            tot = []
+            sq = jnp.zeros((PART, LANES), F32)
+            for t in range(TILES):
+                ls = slice(t * LANES, (t + 1) * LANES)
+                v = base[t, ps, :] + ro2[t, ps, :] * carry[0, cs, ls] + ro3[t, ps, :] * carry[1, cs, ls]
+                sq = sq + v * v
+                tot.append(v)
+            scale = lax.rsqrt(jnp.sum(sq, axis=-1, keepdims=True) * (1.0 / E) + 1e-05)
+            for t in range(TILES):
+                ls = slice(t * LANES, (t + 1) * LANES)
+                nb[r, :, ls] = (tot[t] * scale * gg[t, ps, :]).astype(BF16)
+        res = mxu(nb[...].reshape(R * PART, E), wo[...])
+        at = pl.multiple_of(start + starts[p], PART)
+        ob[:, pl.ds(at, PART), :] = res.astype(BF16).reshape(R, PART, D)
+
+    arrived(2 - 2 * odd)
+    over_chip_part(0)
+    finish(own, cc.at[core], 0)
+    arrived(1)
+    arrived(2 * odd)
+    over_chip_part(1)
+    finish(own, cc.at[core], 1)
+    to_last(near, 0).wait_recv()
+    for p in range(2):
+        last_part(p).wait_recv()
+        finish(other, pc, p)
     for copy in to_core + to_x[0] + to_x[1] + to_cols + to_z + back_copies(near, 0) + back_copies(far, 1):
         copy.wait_send()
     to_last(near, 0).wait_send()
-    to_last(far, 1).wait_send()
+    for p in range(2):
+        last_part(p).wait_send()
 
 
 def local(xin, gate_in, w_proj, rate, skip, norm_gain, w_out):
@@ -487,10 +536,11 @@
         pltpu.VMEM((2, HALF, E), F32),
         pltpu.VMEM((2, R, WIDE), F32),
         pltpu.VMEM((NCOL, R, WIDE), F32),
-        pltpu.VMEM((R, HALF, E), BF16),
+        pltpu.VMEM((R, PART, E), BF16),
         pltpu.SemaphoreType.DMA((7,)),
         pltpu.SemaphoreType.DMA((N_SEM,)),
         pltpu.SemaphoreType.DMA((N_SEM,)),
+        pltpu.SemaphoreType.REGULAR((2,)),
     ]
     return pl.pallas_call(
         kernel,

time: 29.6 us -> 29 us (0.980)
  Pallas kernels: 28.7 us -> 28.1 us
    pallas_call x1, Pallas kernels: 28.7 us -> 28.1 us  [local(): pl.pallas_call(kernel, out_shape=pltpu.VMEM((R, C, D), BF16), in_specs=[h...]
where the time goes in v5:
time: 29 us; the launch traced here: 28.9 us
  Pallas kernels  28.1 us (97%)
  local copies, waits for them, and re-layouts  0.8 us (3%)
    pallas_call x1, Pallas kernels, local(): pl.pallas_call(kernel, out_shape=pltpu.VMEM((R, C, D), BF16), in_specs=[h...  28.1 us
    unnamed x1, local copies, waits for them, and re-layouts  0.8 us

profile of v5, /device:TPU:1, one launch (start us, length us, event | category | flops | bytes accessed | tf_op | source)
XLA Modules:
  0.0 28.9 jit_solution(6933457675796366621)
XLA Ops:
  0.0 28.1 %shard_map.73 = bf16[8,64,512]{2,1,0:T(8,128)(2,1)S(1)} custom-call(bf16[8,64,1024]{2,1,0:T(8,128)(2,1)} %x_hbm.1, bf16[8,64,1024]{2,1,0:T(8,128)(2,1)} %g_hbm.1, bf16[1024,128]{1,0:T(8,128)(2,1)} %wp_hbm.1, f32[4,16]{1,0:T(4,128)} %rate_hbm.1, f32[1,1024]{1,0:T(1,128)} %bitcast.2, f32[1,1024]{1,0:T(1,128)} %bitcast.3, bf16[1024,512]{1,0:T(8,128)(2,1)} %wo_hbm.1), custom_call_target="tpu_custom_call" | custom-call | tf_op jit(solution)/shard_map/pallas_call | solution.py:545
  28.1 0.8 %copy.9 = bf16[8,64,512]{2,1,0:T(8,128)(2,1)} copy(bf16[8,64,512]{2,1,0:T(8,128)(2,1)S(1)} %shard_map.73) | data formatting | bytes 1048576

commit v6 on v5

--- a/solution.py
+++ b/solution.py
@@ -197,6 +197,14 @@
     to_core = [remote(s0.at[i], ee.at[core, i], S_CORE + i, core_peer) for i in range(2)]
     column_ends(other, 1, s0)
 
+    wait_for_core()
+    to_core[1].start()
+    column_ends(other, 0, s0)
+    to_core[0].start()
+    column_ends(own, 1, ee.at[core])
+    column_ends(own, 0, ee.at[core])
+
+
     bt = lax.broadcasted_iota(jnp.int32, (256, 256), 0)
     bs = lax.broadcasted_iota(jnp.int32, (256, 256), 1)
     same = (bt // C) == (bs // C)
@@ -270,14 +278,6 @@
         return 0
 
     lax.fori_loop(0, g_early, gates, 0)
-
-    wait_for_core()
-    to_core[1].start()
-    column_ends(other, 0, s0)
-    to_core[0].start()
-    column_ends(own, 1, ee.at[core])
-    column_ends(own, 0, ee.at[core])
-
 
     to_x = [[remote(tt.at[x_dst[d], i], xe.at[xi, i], S_X + 3 * i + d, x_peers[d]) for d in range(NX - 1)]
             for i in range(2)]
@@ -434,14 +434,14 @@
 
     begin = [in0[:, t * LANES:(t + 1) * LANES] for t in range(TILES)]
     begin += [in1[:, t * LANES:(t + 1) * LANES] for t in range(TILES)]
-    states = lax.fori_loop(0, C // 2, row_step, tuple(begin))
+    states = lax.fori_loop(0, C // 2, row_step, tuple(begin), unroll=2)
 
     @pl.when(jnp.logical_not(edge))
     def _():
         over_groups(near, 0)
 
     over_groups(far, 1)
-    lax.fori_loop(C // 2, C, row_step, states)
+    lax.fori_loop(C // 2, C, row_step, states, unroll=2)
     lax.fori_loop(r_early, CHUNKS, gates, 0)
     lax.fori_loop(r_early, CHUNKS, reach_spread, 0)
     over_chip(near, 0)

time: 29 us -> 28.8 us (level)
  no operation moved by 1% of the time
where the time goes in v6:
time: 28.8 us; the launch traced here: 28.7 us
  Pallas kernels  27.9 us (97%)
  local copies, waits for them, and re-layouts  0.8 us (3%)
    pallas_call x1, Pallas kernels, local(): pl.pallas_call(kernel, out_shape=pltpu.VMEM((R, C, D), BF16), in_specs=[h...  27.9 us
    unnamed x1, local copies, waits for them, and re-layouts  0.8 us

profile of v6, /device:TPU:1, one launch (start us, length us, event | category | flops | bytes accessed | tf_op | source)
XLA Modules:
  0.0 28.7 jit_solution(12188739063884761271)
XLA Ops:
  0.0 27.9 %shard_map.73 = bf16[8,64,512]{2,1,0:T(8,128)(2,1)S(1)} custom-call(bf16[8,64,1024]{2,1,0:T(8,128)(2,1)} %x_hbm.1, bf16[8,64,1024]{2,1,0:T(8,128)(2,1)} %g_hbm.1, bf16[1024,128]{1,0:T(8,128)(2,1)} %wp_hbm.1, f32[4,16]{1,0:T(4,128)} %rate_hbm.1, f32[1,1024]{1,0:T(1,128)} %bitcast.2, f32[1,1024]{1,0:T(1,128)} %bitcast.3, bf16[1024,512]{1,0:T(8,128)(2,1)} %wo_hbm.1), custom_call_target="tpu_custom_call" | custom-call | tf_op jit(solution)/shard_map/pallas_call | solution.py:545
  27.9 0.8 %copy.9 = bf16[8,64,512]{2,1,0:T(8,128)(2,1)} copy(bf16[8,64,512]{2,1,0:T(8,128)(2,1)S(1)} %shard_map.73) | data formatting | bytes 1048576
